TPU v7x, 1024 devices: a whole 8x8x8 slice. The times are simulated.
1024 devices in a mesh: dp: 32 (over y, z_hi, core), expert: 32 (over x, z_lo).
Axes of the slice: x: 8, y: 8, z: 8 (z_hi: 2, z_lo: 4; z = z_hi * 4 + z_lo), core: 2. Of those that a mesh axis runs over, the one named last changes fastest.
Arguments:
- tokens: bfloat16 [2, 8192, 2048], P(None, ('dp', 'expert')), may hold values from -6 to 6
- cotangent: bfloat16 [2, 8192, 2048], P(None, ('dp', 'expert')), may hold values from -6 to 6
- routes: int32 [2, 8192, 2], P(None, ('dp', 'expert')), may hold values from 0 to 15, all different within a row; in each aligned block of 8 rows (0 to 7, 8 to 15, ..., all dimensions but the last counted through in order) at most 2 rows name the same one
- gate_codes: int32 [2, 8192, 2], P(None, ('dp', 'expert')), may hold values from 1 to 255
- gate_weight: bfloat16 [32, 2048, 384], P('expert'), may hold values from -0.125 to 0.125
- up_weight: bfloat16 [32, 2048, 384], P('expert'), may hold values from -0.125 to 0.125
- down_weight: bfloat16 [32, 2048, 384], P('expert'), may hold values from -0.21875 to 0.21875
Outputs:
- mixed: bfloat16 [2, 8192, 2048], P(None, ('dp', 'expert'))
- grad_tokens: bfloat16 [2, 8192, 2048], P(None, ('dp', 'expert'))
- grad_gate: float32 [32, 2048, 384], P('expert', 'dp')
- grad_up: float32 [32, 2048, 384], P('expert', 'dp')
- grad_down: float32 [32, 2048, 384], P('expert', 'dp')
Inputs may be any that keep to these rules, and one draw needn't show every extreme that they name: `routes`: in each micro-batch, the 8 tokens of one device name each expert at most 2 times in all; a token's 2 experts differ.
All inputs are finite; a program needn't handle non-finite values.
Results may differ from a plain program's by a relative error of at most 0.019.
Values may be sent and summed in bfloat16 or wider, within the bound.
A program may use at most 64 MiB of HBM per device.

v0:
```python
import math

import jax
import jax.numpy as jnp
from jax import lax
from jax.sharding import PartitionSpec as P


def slot_tables(route_block, code_block, expert_count, capacity):
    tok_count, top_count = route_block.shape
    flat_routes = route_block.reshape(-1)
    onehot = (flat_routes[:, None] == jnp.arange(expert_count, dtype=jnp.int32)[None, :]).astype(
        jnp.int32
    )
    before = jnp.cumsum(onehot, axis=0) - onehot
    slot_rank = jnp.sum(before * onehot, axis=1)
    slot_place = (slot_rank[:, None] == jnp.arange(capacity, dtype=jnp.int32)[None, :]).astype(
        jnp.float32
    )
    slot_mask = onehot.astype(jnp.float32)[:, :, None] * slot_place[:, None, :]
    slot_mask = slot_mask.reshape(tok_count, top_count, expert_count, capacity)
    code_float = code_block.astype(jnp.float32)
    share_table = code_float / jnp.sum(code_float, axis=1, keepdims=True)
    select = jnp.sum(slot_mask, axis=1)
    gate_share = jnp.sum(share_table[:, :, None, None] * slot_mask, axis=1)
    return (select, gate_share)


def contract_last(left, right):
    return lax.dot_general(
        left, right, (((1,), (1,)), ((), ())), preferred_element_type=jnp.float32
    )


def contract_first(left, right):
    return lax.dot_general(
        left, right, (((0,), (0,)), ((), ())), preferred_element_type=jnp.float32
    )


def expert_pass(slot_rows, slot_cots, w_gate, w_up, w_down):
    pre_gate = jnp.dot(slot_rows, w_gate, preferred_element_type=jnp.float32)
    pre_up = jnp.dot(slot_rows, w_up, preferred_element_type=jnp.float32)
    sigma = jax.nn.sigmoid(pre_gate)
    activ = pre_gate * sigma
    hidden = (activ * pre_up).astype(jnp.bfloat16)
    out_part = contract_last(hidden, w_down).astype(jnp.bfloat16)
    grad_hidden = jnp.dot(slot_cots, w_down, preferred_element_type=jnp.float32)
    grad_pre_gate = (grad_hidden * pre_up * sigma * (1.0 + pre_gate * (1.0 - sigma))).astype(
        jnp.bfloat16
    )
    grad_pre_up = (grad_hidden * activ).astype(jnp.bfloat16)
    grad_in = (contract_last(grad_pre_gate, w_gate) + contract_last(grad_pre_up, w_up)).astype(
        jnp.bfloat16
    )
    return (out_part, grad_in, grad_pre_gate, grad_pre_up, hidden)


def shards(tokens, cotangent, routes, gate_codes, gate_weight, up_weight, down_weight):
    micro_count, tok_count, model_width = tokens.shape
    peer_count = lax.axis_size("expert")
    group_count = lax.axis_size("dp")
    experts = peer_count // 2
    top_count = routes.shape[2]
    capacity = 2 * tok_count * top_count // experts
    scale_factor = 1.0 / math.sqrt(group_count * micro_count * peer_count * capacity)
    w_gate = gate_weight[0]
    w_up = up_weight[0]
    w_down = down_weight[0]
    mixed_list = []
    back_list = []
    rows_saved = []
    cots_saved = []
    gate_saved = []
    up_saved = []
    hidden_saved = []
    for micro_index in range(micro_count):
        select, gate_share = slot_tables(
            routes[micro_index], gate_codes[micro_index], experts, capacity
        )
        select_half = select.astype(jnp.bfloat16)
        send_rows = jnp.einsum(
            "tec,td->ecd", select_half, tokens[micro_index], preferred_element_type=jnp.float32
        )
        send_rows = jnp.broadcast_to(
            send_rows.astype(jnp.bfloat16)[:, None], (experts, 2, capacity, model_width)
        )
        send_rows = send_rows.reshape(peer_count, capacity, model_width)
        slot_share = jnp.sum(gate_share, axis=0)
        cot_slots = jnp.einsum(
            "tec,td->ecd", select_half, cotangent[micro_index], preferred_element_type=jnp.float32
        )
        send_cots = (slot_share[:, :, None] * cot_slots).astype(jnp.bfloat16)
        send_cots = jnp.broadcast_to(send_cots[:, None], (experts, 2, capacity, model_width))
        send_cots = send_cots.reshape(peer_count, capacity, model_width)
        got_rows, got_cots = (
            lax.all_to_all(send_rows, "expert", split_axis=0, concat_axis=0, tiled=True),
            lax.all_to_all(send_cots, "expert", split_axis=0, concat_axis=0, tiled=True),
        )
        slot_rows = got_rows.reshape(peer_count * capacity, model_width)
        slot_cots = got_cots.reshape(peer_count * capacity, model_width)
        out_part, grad_in, grad_pre_gate, grad_pre_up, hidden = expert_pass(
            slot_rows, slot_cots, w_gate, w_up, w_down
        )
        back_out, back_grad = (
            lax.all_to_all(
                out_part.reshape(peer_count, capacity, model_width),
                "expert",
                split_axis=0,
                concat_axis=0,
                tiled=True,
            ),
            lax.all_to_all(
                grad_in.reshape(peer_count, capacity, model_width),
                "expert",
                split_axis=0,
                concat_axis=0,
                tiled=True,
            ),
        )
        out_four = back_out.reshape(experts, 2, capacity, model_width).astype(jnp.float32)
        grad_four = back_grad.reshape(experts, 2, capacity, model_width).astype(jnp.float32)
        out_sum = out_four[:, 0] + out_four[:, 1]
        grad_sum = grad_four[:, 0] + grad_four[:, 1]
        mixed_rows = jnp.einsum("tec,ecd->td", gate_share, out_sum, precision=lax.Precision.HIGHEST)
        back_rows = jnp.einsum("tec,ecd->td", select, grad_sum, precision=lax.Precision.HIGHEST)
        mixed_list.append(mixed_rows.astype(jnp.bfloat16))
        back_list.append(back_rows.astype(jnp.bfloat16))
        rows_saved.append(slot_rows)
        cots_saved.append(slot_cots)
        gate_saved.append(grad_pre_gate)
        up_saved.append(grad_pre_up)
        hidden_saved.append(hidden)
    rows_all = jnp.concatenate(rows_saved, axis=0)
    cots_all = jnp.concatenate(cots_saved, axis=0)
    gate_all = jnp.concatenate(gate_saved, axis=0)
    up_all = jnp.concatenate(up_saved, axis=0)
    hidden_all = jnp.concatenate(hidden_saved, axis=0)
    term_gate = contract_first(rows_all, gate_all) * scale_factor
    term_up = contract_first(rows_all, up_all) * scale_factor
    term_down = contract_first(cots_all, hidden_all) * scale_factor
    grad_gate, grad_up, grad_down = (
        lax.psum_scatter(
            term_gate.astype(jnp.bfloat16), "dp", scatter_dimension=0, tiled=True
        ).astype(jnp.float32),
        lax.psum_scatter(
            term_up.astype(jnp.bfloat16), "dp", scatter_dimension=0, tiled=True
        ).astype(jnp.float32),
        lax.psum_scatter(
            term_down.astype(jnp.bfloat16), "dp", scatter_dimension=0, tiled=True
        ).astype(jnp.float32),
    )
    mixed = jnp.stack(mixed_list)
    grad_tokens = jnp.stack(back_list)
    return (mixed, grad_tokens, grad_gate[None], grad_up[None], grad_down[None])


def solution(mesh):
    in_specs = (
        P(None, ("dp", "expert"), None),
        P(None, ("dp", "expert"), None),
        P(None, ("dp", "expert"), None),
        P(None, ("dp", "expert"), None),
        P("expert", None, None),
        P("expert", None, None),
        P("expert", None, None),
    )
    out_specs = (
        P(None, ("dp", "expert"), None),
        P(None, ("dp", "expert"), None),
        P("expert", "dp", None),
        P("expert", "dp", None),
        P("expert", "dp", None),
    )
    return jax.shard_map(shards, mesh=mesh, in_specs=in_specs, out_specs=out_specs, check_vma=False)
```

profile of v0, /device:TPU:6, one launch (start us, length us, event | category | flops | bytes accessed | tf_op | source)
XLA Modules:
  0.0 545.0 jit_solution(862514592736204263)
XLA Ops:
  12.8 16.9 %all-to-all-start = ((bf16[32,2,2048]{2,1,0:T(2,128)(2,1)}), bf16[32,2,2048]{2,1,0:T(2,128)(2,1)S(1)}, u32[]{:S(2)}, u32[]{:S(2)}) async-start(bf16[32,2,2048]{2,1,0:T(2,128)(2,1)} %bitcast.137), calls=%async_computation | async-start | bytes 524288 | tf_op jit(solution)/shard_map/all_to_all | solution.py:97
  35.0 4.6 all-to-all-done
  39.5 1.9 broadcast_in_dim.24
  41.4 7.3 %all-to-all-start.2 = ((bf16[32,2,2048]{2,1,0:T(2,128)(2,1)}), bf16[32,2,2048]{2,1,0:T(2,128)(2,1)}, u32[]{:S(2)}, u32[]{:S(2)}) async-start(bf16[32,2,2048]{2,1,0:T(2,128)(2,1)} %bitcast.139), calls=%async_computation.2 | async-start | bytes 524288 | tf_op jit(solution)/shard_map/all_to_all | solution.py:97
  52.3 6.1 %all-to-all-done.2 = bf16[32,2,2048]{2,1,0:T(2,128)(2,1)} async-done(((bf16[32,2,2048]{2,1,0:T(2,128)(2,1)}), bf16[32,2,2048]{2,1,0:T(2,128)(2,1)}, u32[]{:S(2)}, u32[]{:S(2)}) %all-to-all-start.2) | async-done | bytes 262176 | tf_op jit(solution)/shard_map/all_to_all | solution.py:97
  58.4 1.8 broadcast_in_dim.25
  60.1 7.2 %all-to-all-start.4 = ((bf16[32,2,2048]{2,1,0:T(2,128)(2,1)}), bf16[32,2,2048]{2,1,0:T(2,128)(2,1)}, u32[]{:S(2)}, u32[]{:S(2)}) async-start(bf16[32,2,2048]{2,1,0:T(2,128)(2,1)} %bitcast.25), calls=%async_computation.4 | async-start | bytes 524288 | tf_op jit(solution)/shard_map/all_to_all | solution.py:98
  71.1 5.9 %all-to-all-done.4 = bf16[32,2,2048]{2,1,0:T(2,128)(2,1)} async-done(((bf16[32,2,2048]{2,1,0:T(2,128)(2,1)}), bf16[32,2,2048]{2,1,0:T(2,128)(2,1)}, u32[]{:S(2)}, u32[]{:S(2)}) %all-to-all-start.4) | async-done | bytes 262176 | tf_op jit(solution)/shard_map/all_to_all | solution.py:98
  77.9 7.2 %all-to-all-start.6 = ((bf16[32,2,2048]{2,1,0:T(2,128)(2,1)}), bf16[32,2,2048]{2,1,0:T(2,128)(2,1)}, u32[]{:S(2)}, u32[]{:S(2)}) async-start(bf16[32,2,2048]{2,1,0:T(2,128)(2,1)} %bitcast.138), calls=%async_computation.6 | async-start | bytes 524288 | tf_op jit(solution)/shard_map/all_to_all | solution.py:98
  85.1 1.7 reshape.217
  87.5 1.9 multiply_convert_fusion.5
  89.5 5.4 all-to-all-done.6
  96.0 2.0 multiply_convert_fusion.3
  97.9 1.8 multiply_convert_fusion.1
  99.8 2.8 multiply_convert_fusion.2
  102.6 2.0 fusion.26
  105.9 1.8 reshape.218
  107.8 7.0 %all-to-all-start.5 = ((bf16[32,2,2048]{2,1,0:T(2,128)(2,1)}), bf16[32,2,2048]{2,1,0:T(2,128)(2,1)}, u32[]{:S(2)}, u32[]{:S(2)}) async-start(bf16[32,2,2048]{2,1,0:T(2,128)(2,1)} %reshape.218), calls=%async_computation.5 | async-start | bytes 524288 | tf_op jit(solution)/shard_map/all_to_all | solution.py:113
  114.8 2.0 fusion.24
  118.1 1.8 reshape.221
  120.0 4.7 all-to-all-done.5
  124.6 6.4 %all-to-all-start.7 = ((bf16[32,2,2048]{2,1,0:T(2,128)(2,1)}), bf16[32,2,2048]{2,1,0:T(2,128)(2,1)S(1)}, u32[]{:S(2)}, u32[]{:S(2)}) async-start(bf16[32,2,2048]{2,1,0:T(2,128)(2,1)} %reshape.221), calls=%async_computation.7 | async-start | bytes 524288 | tf_op jit(solution)/shard_map/all_to_all | solution.py:113
  132.6 8.3 %all-to-all-done.7 = bf16[32,2,2048]{2,1,0:T(2,128)(2,1)S(1)} async-done(((bf16[32,2,2048]{2,1,0:T(2,128)(2,1)}), bf16[32,2,2048]{2,1,0:T(2,128)(2,1)S(1)}, u32[]{:S(2)}, u32[]{:S(2)}) %all-to-all-start.7) | async-done | bytes 262176 | tf_op jit(solution)/shard_map/all_to_all | solution.py:113
  140.8 6.4 %all-to-all-start.1 = ((bf16[32,2,2048]{2,1,0:T(2,128)(2,1)}), bf16[32,2,2048]{2,1,0:T(2,128)(2,1)S(1)}, u32[]{:S(2)}, u32[]{:S(2)}) async-start(bf16[32,2,2048]{2,1,0:T(2,128)(2,1)} %reshape.212), calls=%async_computation.1 | async-start | bytes 524288 | tf_op jit(solution)/shard_map/all_to_all | solution.py:106
  149.0 1.8 multiply_convert_fusion
  152.0 5.1 all-to-all-done.1
  157.0 6.4 %all-to-all-start.3 = ((bf16[32,2,2048]{2,1,0:T(2,128)(2,1)}), bf16[32,2,2048]{2,1,0:T(2,128)(2,1)S(1)}, u32[]{:S(2)}, u32[]{:S(2)}) async-start(bf16[32,2,2048]{2,1,0:T(2,128)(2,1)} %reshape.215), calls=%async_computation.3 | async-start | bytes 524288 | tf_op jit(solution)/shard_map/all_to_all | solution.py:106
  164.3 9.3 %all-to-all-done.3 = bf16[32,2,2048]{2,1,0:T(2,128)(2,1)S(1)} async-done(((bf16[32,2,2048]{2,1,0:T(2,128)(2,1)}), bf16[32,2,2048]{2,1,0:T(2,128)(2,1)S(1)}, u32[]{:S(2)}, u32[]{:S(2)}) %all-to-all-start.3) | async-done | bytes 262176 | tf_op jit(solution)/shard_map/all_to_all | solution.py:106
  177.0 71.5 %reduce-scatter.6.cloned.1.call-done = bf16[64,384]{1,0:T(8,128)(2,1)} async-done(((bf16[2048,384]{1,0:T(8,128)(2,1)}), bf16[64,384]{1,0:T(8,128)(2,1)}) %reduce-scatter.6.cloned.1.call-update) | async-done | bytes 49168 | tf_op jit(solution)/shard_map/reduce_scatter | solution.py:146
  248.5 1.4 bitcast_convert_fusion.1
  249.9 143.3 %reduce-scatter.4.cloned.1.call-done = bf16[64,384]{1,0:T(8,128)(2,1)} async-done(((bf16[2048,384]{1,0:T(8,128)(2,1)}), bf16[64,384]{1,0:T(8,128)(2,1)}) %reduce-scatter.4.cloned.1.call-update) | async-done | bytes 49168 | tf_op jit(solution)/shard_map/reduce_scatter | solution.py:143
  394.7 142.3 %reduce-scatter.8.cloned.1.call-done = bf16[64,384]{1,0:T(8,128)(2,1)} async-done(((bf16[2048,384]{1,0:T(8,128)(2,1)}), bf16[64,384]{1,0:T(8,128)(2,1)}) %reduce-scatter.8.cloned.1.call-update) | async-done | bytes 49168 | tf_op jit(solution)/shard_map/reduce_scatter | solution.py:149
  (107 shorter events, 35.1 us)
Async XLA Ops:
  7.2 80.4 %copy-start = (bf16[1,2048,384]{2,1,0:T(8,128)(2,1)S(1)}, bf16[1,2048,384]{2,1,0:T(8,128)(2,1)}, u32[]{:S(2)}) copy-start(bf16[1,2048,384]{2,1,0:T(8,128)(2,1)} %param.13) | copy-start | bytes 4718596
  7.2 25.6 %copy-start.16 = (bf16[2,8,2048]{2,1,0:T(8,128)(2,1)S(1)}, bf16[2,8,2048]{2,1,0:T(8,128)(2,1)}, u32[]{:S(2)}) copy-start(bf16[2,8,2048]{2,1,0:T(8,128)(2,1)} %param.8) | copy-start | bytes 196612
  10.8 21.9 %copy-start.12 = (f32[8,16,2]{1,0,2:T(8,128)}, f32[8,16,2]{1,0,2:T(8,128)S(1)}, u32[]{:S(2)}) copy-start(f32[8,16,2]{1,0,2:T(8,128)S(1)} %get-tuple-element.9) | copy-start | bytes 3076
  12.8 36.9 %copy-start.1 = (bf16[1,2048,384]{2,1,0:T(8,128)(2,1)S(1)}, bf16[1,2048,384]{2,1,0:T(8,128)(2,1)}, u32[]{:S(2)}) copy-start(bf16[1,2048,384]{2,1,0:T(8,128)(2,1)} %param.12) | copy-start | bytes 4718596
  12.8 26.7 %all-to-all-start = ((bf16[32,2,2048]{2,1,0:T(2,128)(2,1)}), bf16[32,2,2048]{2,1,0:T(2,128)(2,1)S(1)}, u32[]{:S(2)}, u32[]{:S(2)}) async-start(bf16[32,2,2048]{2,1,0:T(2,128)(2,1)} %bitcast.137), calls=%async_computation | async-start | bytes 524288 | tf_op jit(solution)/shard_map/all_to_all | solution.py:97
  32.0 2.2 copy-start.14
  39.5 1.9 copy-start.8
  41.4 17.0 %all-to-all-start.2 = ((bf16[32,2,2048]{2,1,0:T(2,128)(2,1)}), bf16[32,2,2048]{2,1,0:T(2,128)(2,1)}, u32[]{:S(2)}, u32[]{:S(2)}) async-start(bf16[32,2,2048]{2,1,0:T(2,128)(2,1)} %bitcast.139), calls=%async_computation.2 | async-start | bytes 524288 | tf_op jit(solution)/shard_map/all_to_all | solution.py:97
  49.7 2.5 copy-start.4
  49.7 1.5 copy-start.2
  60.1 16.9 %all-to-all-start.4 = ((bf16[32,2,2048]{2,1,0:T(2,128)(2,1)}), bf16[32,2,2048]{2,1,0:T(2,128)(2,1)}, u32[]{:S(2)}, u32[]{:S(2)}) async-start(bf16[32,2,2048]{2,1,0:T(2,128)(2,1)} %bitcast.25), calls=%async_computation.4 | async-start | bytes 524288 | tf_op jit(solution)/shard_map/all_to_all | solution.py:98
  68.4 1.0 copy-start.5
  68.4 1.7 copy-start.3
  77.9 17.0 %all-to-all-start.6 = ((bf16[32,2,2048]{2,1,0:T(2,128)(2,1)}), bf16[32,2,2048]{2,1,0:T(2,128)(2,1)}, u32[]{:S(2)}, u32[]{:S(2)}) async-start(bf16[32,2,2048]{2,1,0:T(2,128)(2,1)} %bitcast.138), calls=%async_computation.6 | async-start | bytes 524288 | tf_op jit(solution)/shard_map/all_to_all | solution.py:98
  85.0 163.5 %reduce-scatter.6.cloned.1.call-start = ((), (), s32[]{:S(2)}) async-start(), calls=%async_computation.12 | async-start | bytes 1622016 | tf_op jit(solution)/shard_map/reduce_scatter | solution.py:146
  95.9 2.0 copy-start.6
  99.7 293.5 %reduce-scatter.4.cloned.1.call-start = ((), (), s32[]{:S(2)}) async-start(), calls=%async_computation.11 | async-start | bytes 1622016 | tf_op jit(solution)/shard_map/reduce_scatter | solution.py:143
  104.6 10.2 %copy-start.9 = (bf16[64,384]{1,0:T(8,128)(2,1)S(1)}, bf16[64,384]{1,0:T(8,128)(2,1)}, u32[]{:S(2)}) copy-start(bf16[64,384]{1,0:T(8,128)(2,1)} %get-tuple-element.17) | copy-start | bytes 147460
  107.8 16.9 %all-to-all-start.5 = ((bf16[32,2,2048]{2,1,0:T(2,128)(2,1)}), bf16[32,2,2048]{2,1,0:T(2,128)(2,1)}, u32[]{:S(2)}, u32[]{:S(2)}) async-start(bf16[32,2,2048]{2,1,0:T(2,128)(2,1)} %reshape.218), calls=%async_computation.5 | async-start | bytes 524288 | tf_op jit(solution)/shard_map/all_to_all | solution.py:113
  116.8 14.2 %copy-start.10 = (bf16[64,384]{1,0:T(8,128)(2,1)S(1)}, bf16[64,384]{1,0:T(8,128)(2,1)}, u32[]{:S(2)}) copy-start(bf16[64,384]{1,0:T(8,128)(2,1)} %get-tuple-element.15) | copy-start | bytes 147460
  124.6 16.2 %all-to-all-start.7 = ((bf16[32,2,2048]{2,1,0:T(2,128)(2,1)}), bf16[32,2,2048]{2,1,0:T(2,128)(2,1)S(1)}, u32[]{:S(2)}, u32[]{:S(2)}) async-start(bf16[32,2,2048]{2,1,0:T(2,128)(2,1)} %reshape.221), calls=%async_computation.7 | async-start | bytes 524288 | tf_op jit(solution)/shard_map/all_to_all | solution.py:113
  131.0 16.4 %copy-start.11 = (bf16[64,384]{1,0:T(8,128)(2,1)S(1)}, bf16[64,384]{1,0:T(8,128)(2,1)}, u32[]{:S(2)}) copy-start(bf16[64,384]{1,0:T(8,128)(2,1)} %get-tuple-element.18) | copy-start | bytes 147460
  132.6 16.4 %copy-start.7 = (bf16[64,2048]{1,0:T(8,128)(2,1)S(1)}, bf16[64,2048]{1,0:T(8,128)(2,1)}, u32[]{:S(2)}) copy-start(bf16[64,2048]{1,0:T(8,128)(2,1)} %reshape.217) | copy-start | bytes 786436
  140.8 16.2 %all-to-all-start.1 = ((bf16[32,2,2048]{2,1,0:T(2,128)(2,1)}), bf16[32,2,2048]{2,1,0:T(2,128)(2,1)S(1)}, u32[]{:S(2)}, u32[]{:S(2)}) async-start(bf16[32,2,2048]{2,1,0:T(2,128)(2,1)} %reshape.212), calls=%async_computation.1 | async-start | bytes 524288 | tf_op jit(solution)/shard_map/all_to_all | solution.py:106
  147.2 389.8 %reduce-scatter.8.cloned.1.call-start = ((), (), s32[]{:S(2)}) async-start(), calls=%async_computation.13 | async-start | bytes 1622016 | tf_op jit(solution)/shard_map/reduce_scatter | solution.py:149
  157.0 16.5 %all-to-all-start.3 = ((bf16[32,2,2048]{2,1,0:T(2,128)(2,1)}), bf16[32,2,2048]{2,1,0:T(2,128)(2,1)S(1)}, u32[]{:S(2)}, u32[]{:S(2)}) async-start(bf16[32,2,2048]{2,1,0:T(2,128)(2,1)} %reshape.215), calls=%async_computation.3 | async-start | bytes 524288 | tf_op jit(solution)/shard_map/all_to_all | solution.py:106
  163.6 10.3 %copy-start.13 = (f32[8,16,2]{1,0,2:T(8,128)S(1)}, f32[8,16,2]{1,0,2:T(8,128)}, u32[]{:S(2)}) copy-start(f32[8,16,2]{1,0,2:T(8,128)} %copy-done.12) | copy-start | bytes 3076
  163.6 10.7 %copy-start.15 = (f32[8,16,2]{1,0,2:T(8,128)S(1)}, f32[8,16,2]{1,0,2:T(8,128)}, u32[]{:S(2)}) copy-start(f32[8,16,2]{1,0,2:T(8,128)} %copy-done.14) | copy-start | bytes 3076
  164.0 10.8 %copy-start.17 = (f32[8,16,2]{1,0,2:T(8,128)S(1)}, f32[8,16,2]{1,0,2:T(8,128)}, u32[]{:S(2)}) copy-start(f32[8,16,2]{1,0,2:T(8,128)} %get-tuple-element.6) | copy-start | bytes 3076
  173.6 1.8 copy-start.18
Sparse Core Ops, SparseCore 0:
  99.9 148.6 reduce-scatter.5
  255.3 137.9 reduce-scatter.3
  399.1 137.8 reduce-scatter.7
where the time goes:
time: 547 us; the launch traced here: 545 us
  waiting for transfers between devices  406 us (74%)
  starting transfers between devices  64.9 us (12%)
  matrix products  26.7 us (5%)
  local copies, waits for them, and re-layouts  21 us (4%)
  between operations  14.2 us (3%)
  other arithmetic  11.6 us (2%)
    reduce_scatter x1, waiting for transfers between devices, shards(): lax.psum_scatter(term_gate.astype(jnp.bfloat16), 'dp', scatter_dimension=...  143 us
    reduce_scatter x1, waiting for transfers between devices, shards(): lax.psum_scatter(term_down.astype(jnp.bfloat16), 'dp', scatter_dimension=...  142 us
    reduce_scatter x1, waiting for transfers between devices, shards(): lax.psum_scatter(term_up.astype(jnp.bfloat16), 'dp', scatter_dimension=0,...  71.5 us
    all_to_all x2, starting transfers between devices, shards(): lax.all_to_all(send_rows, 'expert', split_axis=0, concat_axis=0, tiled=True)  24.1 us
    all_to_all x2, waiting for transfers between devices, shards(): lax.all_to_all(out_part.reshape(peer_count, capacity, model_width), 'expe...  14.3 us
    all_to_all x2, starting transfers between devices, shards(): lax.all_to_all(send_cots, 'expert', split_axis=0, concat_axis=0, tiled=True)  14.3 us
    all_to_all x2, starting transfers between devices, shards(): lax.all_to_all(grad_in.reshape(peer_count, capacity, model_width), 'exper...  13.4 us
    all_to_all x2, waiting for transfers between devices, shards(): lax.all_to_all(grad_in.reshape(peer_count, capacity, model_width), 'exper...  13 us
  transfers between devices with their start and end apart: 11, of which 11 were waited for; matrix products, arithmetic and copies ran while one was open for 8% of the time, Pallas kernels for 0%

commit v1 on v0

v1 whole, which is shorter than its diff:
```python
import functools
import math

import jax
import jax.numpy as jnp
from jax import lax
from jax.experimental import pallas as pl
from jax.experimental.pallas import tpu as pltpu
from jax.sharding import PartitionSpec as P

MESH = pl.DeviceIdType.MESH
F32 = jnp.float32
BF16 = jnp.bfloat16


def dot(left, right):
    return jnp.dot(left, right, preferred_element_type=F32)


def dot_last(left, right):
    return lax.dot_general(left, right, (((1,), (1,)), ((), ())), preferred_element_type=F32)


def dot_first(left, right):
    return lax.dot_general(left, right, (((0,), (0,)), ((), ())), preferred_element_type=F32)


def iota(shape, axis):
    return lax.broadcasted_iota(jnp.int32, shape, axis)


def slot_ranks(cols, lanes):
    width = lanes.shape[1]
    tok_col = iota((16, width), 0)
    tok_lane = iota((16, width), 1) & 15
    same = (tok_col >> 3) == (tok_lane >> 3)
    before = same & (tok_col < tok_lane)
    upto = same & (tok_col <= tok_lane)
    col0, col1 = cols[:, 0:1], cols[:, 1:2]
    lane0, lane1 = lanes[0:1, :], lanes[1:2, :]

    def count(mask):
        return jnp.sum(jnp.where(mask, 1.0, 0.0), axis=0, keepdims=True)

    rank0 = count((col0 == lane0) & before) + count((col1 == lane0) & before)
    rank1 = count((col0 == lane1) & upto) + count((col1 == lane1) & before)
    return rank0, rank1


def slot_masks(rows, shift, cols, lanes):
    width = lanes.shape[1]
    rank0, rank1 = slot_ranks(cols, lanes)
    row = iota((rows, width), 0)
    lane = iota((rows, width), 1)
    expert = row >> shift
    slot = (row & 1).astype(F32)
    fits = (((row >> 2) & 3) == ((lane >> 4) & 3)) & (((row >> 1) & 1) == ((lane >> 3) & 1))
    mask0 = fits & (lanes[0:1, :] == expert) & (rank0 == slot)
    mask1 = fits & (lanes[1:2, :] == expert) & (rank1 == slot)
    return mask0, mask1


def kernel(
    scale_factor,
    n_dp,
    n_peer,
    cols_ref,
    lanes_ref,
    share_ref,
    tok_ref,
    cot_ref,
    wg_hbm,
    wu_hbm,
    wd_hbm,
    mixed_ref,
    back_ref,
    gg_ref,
    gu_ref,
    gd_ref,
    wg,
    wu,
    wd,
    outbox,
    inbox,
    xs,
    xt,
    xt_pair,
    gs,
    gs_pair,
    retbox,
    retin,
    comb,
    parts,
    ring,
    zbox,
    w_sem,
    fs_sem,
    fr_sem,
    rs_sem,
    rr_sem,
    cs_sem,
    cr_sem,
    ys_sem,
    yr_sem,
    zs_sem,
    zr_sem,
):
    k = lax.axis_index("expert")
    i = lax.axis_index("dp")
    n_y = n_dp // 4
    y, zh, core = i // 4, (i // 2) % 2, i % 2
    pair = y * 4 + zh * 2 + (1 - core)
    zpart = y * 4 + (1 - zh) * 2 + core
    up = ((y + 1) % n_y) * 4 + zh * 2 + core
    down = ((y + n_y - 1) % n_y) * 4 + zh * 2 + core

    w_copies = [
        pltpu.make_async_copy(src, dst, w_sem.at[n])
        for n, (src, dst) in enumerate(((wg_hbm, wg), (wu_hbm, wu), (wd_hbm, wd)))
    ]
    for copy in w_copies:
        copy.start()

    barrier = pltpu.get_barrier_semaphore()

    def greet(j, carry):
        pl.semaphore_signal(
            barrier, inc=1, device_id={"expert": (k + j) % n_peer}, device_id_type=MESH
        )
        return carry

    lax.fori_loop(1, n_peer, greet, 0)
    for other in (pair, zpart, up, down):
        pl.semaphore_signal(barrier, inc=1, device_id={"dp": other}, device_id_type=MESH)

    cols = cols_ref[...]
    lanes = lanes_ref[:, 0:64]
    share = share_ref[:, 0:64]
    mask0, mask1 = slot_masks(256, 4, cols, lanes)
    pick = jnp.where(mask0 | mask1, 1.0, 0.0).astype(BF16)
    slot_share = jnp.sum(
        jnp.where(mask0, share[0:1, :], 0.0) + jnp.where(mask1, share[1:2, :], 0.0),
        axis=1,
        keepdims=True,
    )
    is_cot = ((iota((256, 1), 0) >> 2) & 1) == 1
    slot_scale = jnp.where(is_cot, slot_share, 1.0)
    stack = jnp.concatenate(
        [tok_ref[:, 0:1024], cot_ref[:, 0:1024], tok_ref[:, 1024:2048], cot_ref[:, 1024:2048]],
        axis=0,
    )
    outbox[...] = (slot_scale * dot(pick, stack)).astype(BF16).reshape(16, 16, 1024)

    pl.semaphore_wait(barrier, n_peer - 1 + 4)

    def send_copy(j):
        peer = (k + j) % n_peer
        return pltpu.make_async_remote_copy(
            src_ref=outbox.at[peer // 2],
            dst_ref=inbox.at[k],
            send_sem=fs_sem.at[peer],
            recv_sem=fr_sem.at[k],
            device_id={"expert": peer},
            device_id_type=MESH,
        )

    def recv_copy(source):
        return pltpu.make_async_remote_copy(
            src_ref=outbox.at[0],
            dst_ref=inbox.at[source],
            send_sem=fs_sem.at[source],
            recv_sem=fr_sem.at[source],
            device_id={"expert": source},
            device_id_type=MESH,
        )

    def send_start(j, carry):
        send_copy(j).start()
        return carry

    lax.fori_loop(1, n_peer, send_start, 0)
    inbox[k] = outbox[k // 2]

    lanes = lanes_ref[...]
    lane = iota((2, 128), 1)
    weight = jnp.where(((lane >> 4) & 1) == 0, share_ref[...], 1.0)
    high = weight.astype(BF16).astype(F32)
    weight = jnp.where(lane < 64, high, weight - high)
    mask0, mask1 = slot_masks(512, 5, cols, lanes)
    comb[...] = (
        jnp.where(mask0, weight[0:1, :], 0.0) + jnp.where(mask1, weight[1:2, :], 0.0)
    ).astype(BF16)

    def recv_wait(j, carry):
        recv_copy((k + n_peer - j) % n_peer).wait_recv()
        return carry

    lax.fori_loop(1, n_peer, recv_wait, 0)

    row = iota((128, 128), 0)
    lane = iota((128, 128), 1)
    order = jnp.where(((row >> 2) & 7) * 16 + (row >> 5) * 4 + (row & 3) == lane, 1.0, 0.0)
    order = order.astype(BF16)
    for g in range(n_peer // 8):
        block = inbox[g * 8 : (g + 1) * 8].reshape(128, 1024)
        sorted_rows = dot(order, block).astype(BF16)
        for q in range(4):
            xs[q, g * 32 : (g + 1) * 32] = sorted_rows[q * 32 : (q + 1) * 32]

    for q in range(4):
        turned = jnp.transpose(xs[q])
        xt[q % 2, (q // 2) * 8 : (q // 2 + 1) * 8] = turned.reshape(8, 2, 64, 128)
    xt_copy = pltpu.make_async_remote_copy(
        src_ref=xt.at[:, :, 1 - core],
        dst_ref=xt_pair,
        send_sem=cs_sem.at[0],
        recv_sem=cr_sem.at[0],
        device_id={"dp": pair},
        device_id_type=MESH,
    )
    xt_copy.start()

    for copy in w_copies:
        copy.wait()

    pre_gate = dot(xs[0], wg[0:1024]) + dot(xs[2], wg[1024:2048])
    pre_up = dot(xs[0], wu[0:1024]) + dot(xs[2], wu[1024:2048])
    grad_hidden = dot(xs[1], wd[0:1024]) + dot(xs[3], wd[1024:2048])
    sigma = jax.nn.sigmoid(pre_gate)
    activ = pre_gate * sigma
    hidden = (activ * pre_up).astype(BF16)
    grad_gate = (grad_hidden * pre_up * sigma * (1.0 + pre_gate * (1.0 - sigma))).astype(BF16)
    grad_up = (grad_hidden * activ).astype(BF16)
    gs[0] = grad_gate
    gs[1] = grad_up
    gs[2] = hidden
    gs_copy = pltpu.make_async_remote_copy(
        src_ref=gs,
        dst_ref=gs_pair,
        send_sem=cs_sem.at[1],
        recv_sem=cr_sem.at[1],
        device_id={"dp": pair},
        device_id_type=MESH,
    )
    gs_copy.start()

    for d in range(2):
        half = slice(d * 1024, (d + 1) * 1024)
        xs[2 * d] = dot_last(hidden, wd[half]).astype(BF16)
        xs[2 * d + 1] = (dot_last(grad_gate, wg[half]) + dot_last(grad_up, wu[half])).astype(BF16)
    back_order = jnp.where(((lane >> 2) & 7) * 16 + (lane >> 5) * 4 + (lane & 3) == row, 1.0, 0.0)
    back_order = back_order.astype(BF16)
    for g in range(n_peer // 8):
        block = jnp.concatenate([xs[q, g * 32 : (g + 1) * 32] for q in range(4)], axis=0)
        retbox[g * 8 : (g + 1) * 8] = dot(back_order, block).astype(BF16).reshape(8, 16, 1024)

    def ret_copy(j):
        peer = (k + j) % n_peer
        return pltpu.make_async_remote_copy(
            src_ref=retbox.at[peer],
            dst_ref=retin.at[k],
            send_sem=rs_sem.at[peer],
            recv_sem=rr_sem.at[k],
            device_id={"expert": peer},
            device_id_type=MESH,
        )

    def ret_recv(source):
        return pltpu.make_async_remote_copy(
            src_ref=retbox.at[source],
            dst_ref=retin.at[source],
            send_sem=rs_sem.at[source],
            recv_sem=rr_sem.at[source],
            device_id={"expert": source},
            device_id_type=MESH,
        )

    def ret_start(j, carry):
        ret_copy(j).start()
        return carry

    lax.fori_loop(1, n_peer, ret_start, 0)
    retin[k] = retbox[k]

    xt_copy.wait_recv()
    gs_copy.wait_recv()
    for n in range(3):
        a = 0 if n < 2 else 1
        left = jnp.concatenate(
            [xt[a, :, core].reshape(1024, 128), xt_pair[a].reshape(1024, 128)], axis=1
        )
        right = jnp.concatenate([gs[n], gs_pair[n]], axis=0)
        part = (dot(left, right) * scale_factor).astype(BF16)
        parts[:, n * 64 : (n + 1) * 64] = part.reshape(16, 64, 384)

    streams = [(part_at, d) for part_at in range(2) for d in range(2)]

    def own_piece(part_at, d, step):
        side = 1 - zh if part_at == 0 else zh
        at = (y + 2 * n_y - 1 - step) % n_y if d == 0 else (y + 1 + step) % n_y
        return parts.at[at * 2 + side, pl.ds(d * 96, 96)]

    def ring_copy(n, source, step):
        return pltpu.make_async_remote_copy(
            src_ref=source,
            dst_ref=ring.at[n, step],
            send_sem=ys_sem.at[n, step],
            recv_sem=yr_sem.at[n, step],
            device_id={"dp": up if streams[n][1] == 0 else down},
            device_id_type=MESH,
        )

    for n, (part_at, d) in enumerate(streams):
        ring_copy(n, own_piece(part_at, d, 0), 0).start()

    def ring_add(n, step):
        part_at, d = streams[n]
        ring_copy(n, ring.at[n, step], step).wait_recv()
        ring[n, step] = (
            ring[n, step].astype(F32) + own_piece(part_at, d, step + 1)[...].astype(F32)
        ).astype(BF16)

    def ring_step(step, carry):
        for n in range(4):
            ring_add(n, step)
            ring_copy(n, ring.at[n, step], step + 1).start()
        return carry

    last = n_y - 2
    lax.fori_loop(0, last, ring_step, 0)

    z_copies = [
        pltpu.make_async_remote_copy(
            src_ref=ring.at[d, last],
            dst_ref=zbox.at[d],
            send_sem=zs_sem.at[d],
            recv_sem=zr_sem.at[d],
            device_id={"dp": zpart},
            device_id_type=MESH,
        )
        for d in range(2)
    ]
    for d in range(2):
        ring_add(d, last)
        z_copies[d].start()

    def ret_wait(j, carry):
        ret_recv((k + n_peer - j) % n_peer).wait_recv()
        return carry

    lax.fori_loop(1, n_peer, ret_wait, 0)
    both = dot_first(comb[...], retin[...].reshape(512, 1024))
    total = (both[0:64] + both[64:128]).astype(BF16)
    mixed_ref[:, 0:1024] = total[0:16]
    back_ref[:, 0:1024] = total[16:32]
    mixed_ref[:, 1024:2048] = total[32:48]
    back_ref[:, 1024:2048] = total[48:64]

    sums = []
    for d in range(2):
        n = 2 + d
        ring_copy(n, ring.at[n, last], last).wait_recv()
        own = ring[n, last].astype(F32) + own_piece(1, d, last + 1)[...].astype(F32)
        z_copies[d].wait_recv()
        sums.append(own + zbox[d].astype(F32))
    gg_ref[...] = sums[0][0:64]
    gu_ref[0:32] = sums[0][64:96]
    gu_ref[32:64] = sums[1][0:32]
    gd_ref[...] = sums[1][32:96]

    def send_wait(j, carry):
        send_copy(j).wait_send()
        ret_copy(j).wait_send()
        return carry

    lax.fori_loop(1, n_peer, send_wait, 0)
    xt_copy.wait_send()
    gs_copy.wait_send()

    def ring_wait(step, carry):
        for n in range(4):
            ring_copy(n, ring.at[n, step], step).wait_send()
        return carry

    lax.fori_loop(0, last + 1, ring_wait, 0)
    for copy in z_copies:
        copy.wait_send()


def shards(tokens, cotangent, routes, gate_codes, gate_weight, up_weight, down_weight):
    micro, toks, width = tokens.shape
    n_peer = lax.axis_size("expert")
    n_dp = lax.axis_size("dp")
    hidden = gate_weight.shape[2]
    rows = micro * toks
    scale_factor = 1.0 / math.sqrt(n_dp * micro * n_peer * 2)
    cols = routes.reshape(rows, 2)
    codes = gate_codes.reshape(rows, 2).astype(F32)
    share = codes / jnp.sum(codes, axis=1, keepdims=True)
    lanes = jnp.tile(cols.T, (1, 8))
    share = jnp.tile(share.T, (1, 8))
    n_y = n_dp // 4
    vmem = pl.BlockSpec(memory_space=pltpu.VMEM)
    anyspace = pl.BlockSpec(memory_space=pl.ANY)
    dma = pltpu.SemaphoreType.DMA
    grad = jax.ShapeDtypeStruct((width // n_dp, hidden), F32)
    mixed, back, gg, gu, gd = pl.pallas_call(
        functools.partial(kernel, scale_factor, n_dp, n_peer),
        out_shape=(
            jax.ShapeDtypeStruct((rows, width), BF16),
            jax.ShapeDtypeStruct((rows, width), BF16),
            grad,
            grad,
            grad,
        ),
        in_specs=[vmem] * 5 + [anyspace] * 3,
        out_specs=(vmem,) * 5,
        scratch_shapes=[
            pltpu.VMEM((width, hidden), BF16),
            pltpu.VMEM((width, hidden), BF16),
            pltpu.VMEM((width, hidden), BF16),
            pltpu.VMEM((n_peer // 2, 16, 1024), BF16),
            pltpu.VMEM((n_peer, 16, 1024), BF16),
            pltpu.VMEM((4, 128, 1024), BF16),
            pltpu.VMEM((2, 16, 2, 64, 128), BF16),
            pltpu.VMEM((2, 16, 64, 128), BF16),
            pltpu.VMEM((3, 128, hidden), BF16),
            pltpu.VMEM((3, 128, hidden), BF16),
            pltpu.VMEM((n_peer, 16, 1024), BF16),
            pltpu.VMEM((n_peer, 16, 1024), BF16),
            pltpu.VMEM((512, 128), BF16),
            pltpu.VMEM((16, 192, hidden), BF16),
            pltpu.VMEM((4, n_y - 1, 96, hidden), BF16),
            pltpu.VMEM((2, 96, hidden), BF16),
            dma((3,)),
            dma((n_peer,)),
            dma((n_peer,)),
            dma((n_peer,)),
            dma((n_peer,)),
            dma((2,)),
            dma((2,)),
            dma((4, n_y - 1)),
            dma((4, n_y - 1)),
            dma((2,)),
            dma((2,)),
        ],
        compiler_params=pltpu.CompilerParams(
            collective_id=0, has_side_effects=True, vmem_limit_bytes=48 * 1024 * 1024
        ),
        name="moe_layer",
    )(
        cols,
        lanes,
        share,
        tokens.reshape(rows, width),
        cotangent.reshape(rows, width),
        gate_weight[0],
        up_weight[0],
        down_weight[0],
    )
    shape = (micro, toks, width)
    return mixed.reshape(shape), back.reshape(shape), gg[None], gu[None], gd[None]


def solution(mesh):
    tok_spec = P(None, ("dp", "expert"), None)
    w_spec = P("expert", None, None)
    g_spec = P("expert", "dp", None)
    return jax.shard_map(
        shards,
        mesh=mesh,
        in_specs=(tok_spec,) * 4 + (w_spec,) * 3,
        out_specs=(tok_spec,) * 2 + (g_spec,) * 3,
        check_vma=False,
    )
```

time: 547 us -> 108 us (0.20)
  the two profiles are of different devices: /device:TPU:6 before, /device:TPU:8 now
where the time goes in v1:
time: 108 us; the launch traced here: 107 us
  Pallas kernels  95 us (88%)
  local copies, waits for them, and re-layouts  10.3 us (10%)
  other arithmetic  1.39 us (1%)
    pallas_call x1, Pallas kernels, shards(): pl.pallas_call(functools.partial(kernel, scale_factor, n_dp, n_peer), out...  95 us
    unnamed x16, local copies, waits for them, and re-layouts  9.77 us

profile of v1, /device:TPU:8, one launch (start us, length us, event | category | flops | bytes accessed | tf_op | source)
XLA Modules:
  0.0 107.3 jit_solution(8718078710288700265)
XLA Ops:
  0.6 0.7 convert_reduce_fusion
  1.3 0.1 div.10
  1.4 0.7 copy.12
  2.1 0.1 reshape.38
  2.2 0.7 convert_element_type.7
  2.9 0.1 convert_element_type.8
  3.0 0.1 tile.21.share_ref
  3.1 0.1 tile.9.lanes_ref
  3.1 0.1 copy.14.cols_ref
  3.2 0.0 copy-start
  3.2 1.4 %copy-done = bf16[1,2048,384]{2,1,0:T(8,128)(2,1)S(1)} copy-done((bf16[1,2048,384]{2,1,0:T(8,128)(2,1)S(1)}, bf16[1,2048,384]{2,1,0:T(8,128)(2,1)}, u32[]{:S(2)}) %copy-start) | copy-done | bytes 1572888
  4.6 0.0 copy-start.1
  4.6 1.4 %copy-done.1 = bf16[1,2048,384]{2,1,0:T(8,128)(2,1)S(1)} copy-done((bf16[1,2048,384]{2,1,0:T(8,128)(2,1)S(1)}, bf16[1,2048,384]{2,1,0:T(8,128)(2,1)}, u32[]{:S(2)}) %copy-start.1) | copy-done | bytes 1572888
  6.0 0.0 copy-start.2
  6.0 1.4 %copy-done.2 = bf16[1,2048,384]{2,1,0:T(8,128)(2,1)S(1)} copy-done((bf16[1,2048,384]{2,1,0:T(8,128)(2,1)S(1)}, bf16[1,2048,384]{2,1,0:T(8,128)(2,1)}, u32[]{:S(2)}) %copy-start.2) | copy-done | bytes 1572888
  7.5 0.0 copy-start.3
  7.5 0.8 copy-done.3
  8.3 0.0 copy-start.4
  8.3 0.8 copy-done.4
  9.1 95.0 %moe_layer.1 = (bf16[16,2048]{1,0:T(8,128)(2,1)S(1)}, bf16[16,2048]{1,0:T(8,128)(2,1)S(1)}, f32[64,384]{1,0:T(8,128)S(1)}, f32[64,384]{1,0:T(8,128)S(1)}, f32[64,384]{1,0:T(8,128)S(1)}) custom-call(s32[16,2]{1,0:T(8,128)S(1)} %copy.14.cols_ref, s32[2,128]{1,0:T(2,128)S(1)} %tile.9.lanes_ref, f32[2,128]{1,0:T(2,128)S(1)} %tile.21.share_ref, ...), custom_call_target="tpu_custom_call" | custom-call | tf_op jit(solution)/shard_map/moe_layer/pallas_call | solution.py:407
  104.1 0.6 copy.20
  104.8 0.6 copy.21
  105.4 0.6 copy.22
  106.0 0.6 copy.23
  106.7 0.6 copy.24
  (4 shorter events, 0.0 us)
Async XLA Ops:
  3.2 1.4 %copy-start = (bf16[1,2048,384]{2,1,0:T(8,128)(2,1)S(1)}, bf16[1,2048,384]{2,1,0:T(8,128)(2,1)}, u32[]{:S(2)}) copy-start(bf16[1,2048,384]{2,1,0:T(8,128)(2,1)} %param.11) | copy-start | bytes 4718596
  4.6 1.4 %copy-start.1 = (bf16[1,2048,384]{2,1,0:T(8,128)(2,1)S(1)}, bf16[1,2048,384]{2,1,0:T(8,128)(2,1)}, u32[]{:S(2)}) copy-start(bf16[1,2048,384]{2,1,0:T(8,128)(2,1)} %param.12) | copy-start | bytes 4718596
  6.0 1.4 %copy-start.2 = (bf16[1,2048,384]{2,1,0:T(8,128)(2,1)S(1)}, bf16[1,2048,384]{2,1,0:T(8,128)(2,1)}, u32[]{:S(2)}) copy-start(bf16[1,2048,384]{2,1,0:T(8,128)(2,1)} %param.13) | copy-start | bytes 4718596
  7.5 0.8 copy-start.3
  8.3 0.8 copy-start.4

commit v2 on v1

v2 whole, which is shorter than its diff:
```python
import functools
import math

import jax
import jax.numpy as jnp
from jax import lax
from jax.experimental import pallas as pl
from jax.experimental.pallas import tpu as pltpu
from jax.sharding import PartitionSpec as P

MESH = pl.DeviceIdType.MESH
F32 = jnp.float32
BF16 = jnp.bfloat16

ORDER = (0, 1, 7, 2, 6, 3, 5, 4)


def dot(left, right):
    return jnp.dot(left, right, preferred_element_type=F32)


def dot_last(left, right):
    return lax.dot_general(left, right, (((1,), (1,)), ((), ())), preferred_element_type=F32)


def dot_first(left, right):
    return lax.dot_general(left, right, (((0,), (0,)), ((), ())), preferred_element_type=F32)


def iota(shape, axis):
    return lax.broadcasted_iota(jnp.int32, shape, axis)


def route_vectors(route_ref, code_ref):
    row = iota((16, 8), 0)
    lane = iota((16, 8), 1)
    here = [(lane == (row & 7)) & ((row >> 3) == m) for m in range(2)]

    def column(ref, r):
        parts = [jnp.where(here[m], ref[m, r : r + 1, :].astype(F32), 0.0) for m in range(2)]
        return jnp.sum(parts[0] + parts[1], axis=1, keepdims=True)

    spread = iota((16, 128), 0) == (iota((16, 128), 1) & 15)

    def along(col):
        return jnp.sum(jnp.where(spread, col, 0.0), axis=0, keepdims=True)

    cols = [column(route_ref, r) for r in range(2)]
    codes = [column(code_ref, r) for r in range(2)]
    whole = codes[0] + codes[1]
    lanes = jnp.concatenate([along(col) for col in cols], axis=0)
    share = jnp.concatenate([along(code / whole) for code in codes], axis=0)
    return jnp.concatenate(cols, axis=1), lanes, share


def slot_ranks(cols, lanes):
    width = lanes.shape[1]
    tok_col = iota((16, width), 0)
    tok_lane = iota((16, width), 1) & 15
    same = (tok_col >> 3) == (tok_lane >> 3)
    before = same & (tok_col < tok_lane)
    upto = same & (tok_col <= tok_lane)
    col0, col1 = cols[:, 0:1], cols[:, 1:2]
    lane0, lane1 = lanes[0:1, :], lanes[1:2, :]

    def count(mask):
        return jnp.sum(jnp.where(mask, 1.0, 0.0), axis=0, keepdims=True)

    rank0 = count((col0 == lane0) & before) + count((col1 == lane0) & before)
    rank1 = count((col0 == lane1) & upto) + count((col1 == lane1) & before)
    return rank0, rank1


def slot_masks(rows, shift, cols, lanes):
    width = lanes.shape[1]
    rank0, rank1 = slot_ranks(cols, lanes)
    row = iota((rows, width), 0)
    lane = iota((rows, width), 1)
    expert = (row >> shift).astype(F32)
    slot = (row & 1).astype(F32)
    fits = (((row >> 2) & 3) == ((lane >> 4) & 3)) & (((row >> 1) & 1) == ((lane >> 3) & 1))
    mask0 = fits & (lanes[0:1, :] == expert) & (rank0 == slot)
    mask1 = fits & (lanes[1:2, :] == expert) & (rank1 == slot)
    return mask0, mask1


def kernel(
    scale_factor,
    n_dp,
    n_peer,
    route_hbm,
    code_hbm,
    tok_hbm,
    cot_hbm,
    wg_hbm,
    wu_hbm,
    wd_hbm,
    mixed_ref,
    back_ref,
    gg_ref,
    gu_ref,
    gd_ref,
    route_ref,
    code_ref,
    tok_ref,
    cot_ref,
    wg,
    wu,
    wd,
    outbox,
    relay,
    inbox,
    xs,
    xt,
    xt_pair,
    gs,
    gs_pair,
    retbox,
    retin,
    comb,
    parts,
    ring,
    zbox,
    w_sem,
    xs_sem,
    xr_sem,
    ps_sem,
    os_sem,
    hs_sem,
    pr_sem,
    rs_sem,
    rr_sem,
    cs_sem,
    cr_sem,
    ys_sem,
    yr_sem,
    zs_sem,
    zr_sem,
):
    k = lax.axis_index("expert")
    i = lax.axis_index("dp")
    n_y = n_dp // 4
    n_x = n_peer // 4
    x, z = k // 4, k % 4
    y, zh, core = i // 4, (i // 2) % 2, i % 2
    pair = y * 4 + zh * 2 + (1 - core)
    zpart = y * 4 + (1 - zh) * 2 + core
    up = ((y + 1) % n_y) * 4 + zh * 2 + core
    down = ((y + n_y - 1) % n_y) * 4 + zh * 2 + core

    loads = (
        (route_hbm, route_ref),
        (code_hbm, code_ref),
        (tok_hbm, tok_ref),
        (cot_hbm, cot_ref),
        (wg_hbm.at[0], wg),
        (wu_hbm.at[0], wu),
        (wd_hbm.at[0], wd),
    )
    loads = [pltpu.make_async_copy(src, dst, w_sem.at[n]) for n, (src, dst) in enumerate(loads)]
    t_copies, w_copies = loads[:4], loads[4:]
    for copy in loads:
        copy.start()

    barrier = pltpu.get_barrier_semaphore()

    def greet(j, carry):
        pl.semaphore_signal(
            barrier, inc=1, device_id={"expert": (k + j) % n_peer}, device_id_type=MESH
        )
        return carry

    lax.fori_loop(1, n_peer, greet, 0)
    for other in (pair, zpart, up, down):
        pl.semaphore_signal(barrier, inc=1, device_id={"dp": other}, device_id_type=MESH)

    for copy in t_copies:
        copy.wait()

    cols, all_lanes, all_share = route_vectors(route_ref, code_ref)
    lanes = all_lanes[:, 0:64]
    share = all_share[:, 0:64]
    mask0, mask1 = slot_masks(256, 4, cols, lanes)
    pick = jnp.where(mask0 | mask1, 1.0, 0.0).astype(BF16)
    slot_share = jnp.sum(
        jnp.where(mask0, share[0:1, :], 0.0) + jnp.where(mask1, share[1:2, :], 0.0),
        axis=1,
        keepdims=True,
    )
    is_cot = ((iota((256, 1), 0) >> 2) & 1) == 1
    slot_scale = jnp.where(is_cot, slot_share, 1.0)
    stack = jnp.concatenate(
        [
            ref[m, :, d * 1024 : (d + 1) * 1024]
            for d in range(2)
            for ref in (tok_ref, cot_ref)
            for m in range(2)
        ],
        axis=0,
    )
    outbox[...] = (slot_scale * dot(pick, stack)).astype(BF16).reshape(16, 16, 1024)

    pl.semaphore_wait(barrier, n_peer - 1 + 4)

    def over_x(at):
        return pltpu.make_async_remote_copy(
            src_ref=outbox.at[pl.ds((x + ORDER[at]) % n_x * 2, 2)],
            dst_ref=relay.at[at],
            send_sem=xs_sem.at[at],
            recv_sem=xr_sem.at[at],
            device_id={"expert": (x + ORDER[at]) % n_x * 4 + z},
            device_id_type=MESH,
        )

    def to_pair(at):
        return pltpu.make_async_remote_copy(
            src_ref=relay.at[at, z // 2],
            dst_ref=inbox.at[at, z],
            send_sem=ps_sem.at[at],
            recv_sem=pr_sem.at[at, z],
            device_id={"expert": x * 4 + z + 1 - z % 2 * 2},
            device_id_type=MESH,
        )

    def to_other(at):
        return pltpu.make_async_remote_copy(
            src_ref=relay.at[at, 1 - z // 2],
            dst_ref=inbox.at[at, z],
            send_sem=os_sem.at[at],
            recv_sem=pr_sem.at[at, z],
            device_id={"expert": x * 4 + (1 - z // 2) * 2 + at % 2},
            device_id_type=MESH,
        )

    def hand_on(turn, b):
        at = turn * 2 + z % 2
        source = (1 - z // 2) * 2 + b
        return pltpu.make_async_remote_copy(
            src_ref=inbox.at[at, source],
            dst_ref=inbox.at[at, source],
            send_sem=hs_sem.at[turn, b],
            recv_sem=pr_sem.at[at, source],
            device_id={"expert": x * 4 + z + 1 - z % 2 * 2},
            device_id_type=MESH,
        )

    def arrival(at, source):
        return pltpu.make_async_remote_copy(
            src_ref=inbox.at[at, source],
            dst_ref=inbox.at[at, source],
            send_sem=ps_sem.at[0],
            recv_sem=pr_sem.at[at, source],
            device_id={"expert": x * 4 + z + 1 - z % 2 * 2},
            device_id_type=MESH,
        )

    for at in range(1, n_x):
        over_x(at).start()
    relay[0] = outbox[pl.ds(x * 2, 2)]

    lane = iota((2, 128), 1)
    weight = jnp.where(((lane >> 4) & 1) == 0, all_share, 1.0)
    high = weight.astype(BF16).astype(F32)
    weight = jnp.where(lane < 64, high, weight - high)
    mask0, mask1 = slot_masks(512, 5, cols, all_lanes)
    comb[...] = (
        jnp.where(mask0, weight[0:1, :], 0.0) + jnp.where(mask1, weight[1:2, :], 0.0)
    ).astype(BF16)

    row = iota((128, 128), 0)
    lane = iota((128, 128), 1)
    order = jnp.where(((row >> 2) & 7) * 16 + (row >> 5) * 4 + (row & 3) == lane, 1.0, 0.0)
    order = order.astype(BF16)

    def forward(at):
        if at:
            over_x(at).wait_recv()
        to_pair(at).start()
        to_other(at).start()
        inbox[at, z] = relay[at, z // 2]

    def relay_turn(turn):
        for b in range(2):
            arrival(turn * 2 + z % 2, (1 - z // 2) * 2 + b).wait_recv()
            hand_on(turn, b).start()

    def sort_rows(g):
        for at in (2 * g, 2 * g + 1):
            arrival(at, z + 1 - z % 2 * 2).wait_recv()
        for b in range(2):
            arrival(2 * g + 1 - z % 2, (1 - z // 2) * 2 + b).wait_recv()
        block = inbox[2 * g : 2 * g + 2].reshape(128, 1024)
        sorted_rows = dot(order, block).astype(BF16)
        for q in range(4):
            xs[q, g * 32 : (g + 1) * 32] = sorted_rows[q * 32 : (q + 1) * 32]

    forward(0)
    forward(1)
    forward(2)
    relay_turn(0)
    forward(3)
    forward(4)
    relay_turn(1)
    forward(5)
    forward(6)
    relay_turn(2)
    sort_rows(0)
    forward(7)
    sort_rows(1)
    relay_turn(3)
    sort_rows(2)
    sort_rows(3)

    for copy in w_copies:
        copy.wait()

    pre_gate = dot(xs[0], wg[0:1024]) + dot(xs[2], wg[1024:2048])
    pre_up = dot(xs[0], wu[0:1024]) + dot(xs[2], wu[1024:2048])
    grad_hidden = dot(xs[1], wd[0:1024]) + dot(xs[3], wd[1024:2048])
    sigma = jax.nn.sigmoid(pre_gate)
    activ = pre_gate * sigma
    hidden = (activ * pre_up).astype(BF16)
    grad_gate = (grad_hidden * pre_up * sigma * (1.0 + pre_gate * (1.0 - sigma))).astype(BF16)
    grad_up = (grad_hidden * activ).astype(BF16)
    gs[0] = grad_gate
    gs[1] = grad_up
    gs[2] = hidden
    gs_copy = pltpu.make_async_remote_copy(
        src_ref=gs,
        dst_ref=gs_pair,
        send_sem=cs_sem.at[1],
        recv_sem=cr_sem.at[1],
        device_id={"dp": pair},
        device_id_type=MESH,
    )
    gs_copy.start()

    for q in range(4):
        turned = jnp.transpose(xs[q])
        xt[q % 2, (q // 2) * 8 : (q // 2 + 1) * 8] = turned.reshape(8, 2, 64, 128)
    xt_copy = pltpu.make_async_remote_copy(
        src_ref=xt.at[:, :, 1 - core],
        dst_ref=xt_pair,
        send_sem=cs_sem.at[0],
        recv_sem=cr_sem.at[0],
        device_id={"dp": pair},
        device_id_type=MESH,
    )
    xt_copy.start()

    xt_copy.wait_recv()
    gs_copy.wait_recv()
    for n in range(3):
        a = 0 if n < 2 else 1
        left = jnp.concatenate(
            [xt[a, :, core].reshape(1024, 128), xt_pair[a].reshape(1024, 128)], axis=1
        )
        right = jnp.concatenate([gs[n], gs_pair[n]], axis=0)
        part = (dot(left, right) * scale_factor).astype(BF16)
        parts[:, n * 64 : (n + 1) * 64] = part.reshape(16, 64, 384)

    streams = [(part_at, d) for part_at in range(2) for d in range(2)]

    def own_piece(part_at, d, step):
        side = 1 - zh if part_at == 0 else zh
        at = (y + 2 * n_y - 1 - step) % n_y if d == 0 else (y + 1 + step) % n_y
        return parts.at[at * 2 + side, pl.ds(d * 96, 96)]

    def ring_copy(n, source, step):
        return pltpu.make_async_remote_copy(
            src_ref=source,
            dst_ref=ring.at[n, step],
            send_sem=ys_sem.at[n, step],
            recv_sem=yr_sem.at[n, step],
            device_id={"dp": up if streams[n][1] == 0 else down},
            device_id_type=MESH,
        )

    for n, (part_at, d) in enumerate(streams):
        ring_copy(n, own_piece(part_at, d, 0), 0).start()

    for d in range(2):
        half = slice(d * 1024, (d + 1) * 1024)
        xs[2 * d] = dot_last(hidden, wd[half]).astype(BF16)
        xs[2 * d + 1] = (dot_last(grad_gate, wg[half]) + dot_last(grad_up, wu[half])).astype(BF16)
    back_order = jnp.where(((lane >> 2) & 7) * 16 + (lane >> 5) * 4 + (lane & 3) == row, 1.0, 0.0)
    back_order = back_order.astype(BF16)
    for g in range(n_peer // 8):
        block = jnp.concatenate([xs[q, g * 32 : (g + 1) * 32] for q in range(4)], axis=0)
        retbox[2 * g : 2 * g + 2] = dot(back_order, block).astype(BF16).reshape(2, 4, 16, 1024)

    def ret_copy(at, source):
        return pltpu.make_async_remote_copy(
            src_ref=retbox.at[at, source],
            dst_ref=retin.at[k],
            send_sem=rs_sem.at[at, source],
            recv_sem=rr_sem.at[k],
            device_id={"expert": (x + n_x - ORDER[at]) % n_x * 4 + source},
            device_id_type=MESH,
        )

    def ret_recv(source):
        return pltpu.make_async_remote_copy(
            src_ref=retin.at[source],
            dst_ref=retin.at[source],
            send_sem=rs_sem.at[0, 0],
            recv_sem=rr_sem.at[source],
            device_id={"expert": source},
            device_id_type=MESH,
        )

    def ret_sends():
        return [(0, (z + n) % 4) for n in range(1, 4)] + [
            (at, (z + n) % 4) for at in range(1, n_x) for n in range(4)
        ]

    for at, source in ret_sends():
        ret_copy(at, source).start()
    retin[k] = retbox[0, z]

    def ring_add(n, step):
        part_at, d = streams[n]
        ring_copy(n, ring.at[n, step], step).wait_recv()
        ring[n, step] = (
            ring[n, step].astype(F32) + own_piece(part_at, d, step + 1)[...].astype(F32)
        ).astype(BF16)

    def ring_step(step, carry):
        for n in range(4):
            ring_add(n, step)
            ring_copy(n, ring.at[n, step], step + 1).start()
        return carry

    last = n_y - 2
    lax.fori_loop(0, last, ring_step, 0)

    z_copies = [
        pltpu.make_async_remote_copy(
            src_ref=ring.at[d, last],
            dst_ref=zbox.at[d],
            send_sem=zs_sem.at[d],
            recv_sem=zr_sem.at[d],
            device_id={"dp": zpart},
            device_id_type=MESH,
        )
        for d in range(2)
    ]
    for d in range(2):
        ring_add(d, last)
        z_copies[d].start()

    def ret_wait(j, carry):
        ret_recv((k + n_peer - j) % n_peer).wait_recv()
        return carry

    lax.fori_loop(1, n_peer, ret_wait, 0)
    both = dot_first(comb[...], retin[...].reshape(512, 1024))
    total = (both[0:64] + both[64:128]).astype(BF16)
    for m in range(2):
        for d in range(2):
            half = slice(d * 1024, (d + 1) * 1024)
            at = d * 32 + m * 8
            mixed_ref[m, :, half] = total[at : at + 8]
            back_ref[m, :, half] = total[at + 16 : at + 24]

    sums = []
    for d in range(2):
        n = 2 + d
        ring_copy(n, ring.at[n, last], last).wait_recv()
        own = ring[n, last].astype(F32) + own_piece(1, d, last + 1)[...].astype(F32)
        z_copies[d].wait_recv()
        sums.append(own + zbox[d].astype(F32))
    gg_ref[0] = sums[0][0:64]
    gu_ref[0, 0:32] = sums[0][64:96]
    gu_ref[0, 32:64] = sums[1][0:32]
    gd_ref[0] = sums[1][32:96]

    for at in range(n_x):
        if at:
            over_x(at).wait_send()
        to_pair(at).wait_send()
        to_other(at).wait_send()
    for turn in range(n_x // 2):
        for b in range(2):
            hand_on(turn, b).wait_send()
    for at, source in ret_sends():
        ret_copy(at, source).wait_send()
    xt_copy.wait_send()
    gs_copy.wait_send()

    def ring_wait(step, carry):
        for n in range(4):
            ring_copy(n, ring.at[n, step], step).wait_send()
        return carry

    lax.fori_loop(0, last + 1, ring_wait, 0)
    for copy in z_copies:
        copy.wait_send()


def write_kernel(count, *refs):
    ins, outs, held = refs[:count], refs[count : 2 * count], refs[2 * count : 3 * count]
    in_sem, out_sem = refs[3 * count :]
    reads = [pltpu.make_async_copy(ins[n], held[n], in_sem.at[n]) for n in range(count)]
    writes = [pltpu.make_async_copy(held[n], outs[n], out_sem.at[n]) for n in range(count)]
    for copy in reads:
        copy.start()
    for n in range(count):
        reads[n].wait()
        writes[n].start()
    for copy in writes:
        copy.wait()


def shards(tokens, cotangent, routes, gate_codes, gate_weight, up_weight, down_weight):
    micro, toks, width = tokens.shape
    n_peer = lax.axis_size("expert")
    n_dp = lax.axis_size("dp")
    hidden = gate_weight.shape[2]
    scale_factor = 1.0 / math.sqrt(n_dp * micro * n_peer * 2)
    n_y = n_dp // 4
    n_x = n_peer // 4
    vmem = pl.BlockSpec(memory_space=pltpu.VMEM)
    hbm = pl.BlockSpec(memory_space=pltpu.HBM)
    anyspace = pl.BlockSpec(memory_space=pl.ANY)
    dma = pltpu.SemaphoreType.DMA
    tok = jax.ShapeDtypeStruct((micro, toks, width), BF16)
    grad = jax.ShapeDtypeStruct((1, width // n_dp, hidden), F32)
    shapes = (tok, tok, grad, grad, grad)
    results = pl.pallas_call(
        functools.partial(kernel, scale_factor, n_dp, n_peer),
        out_shape=shapes,
        in_specs=[hbm] * 7,
        out_specs=(vmem,) * 5,
        scratch_shapes=[
            pltpu.VMEM((micro, 2, toks), jnp.int32),
            pltpu.VMEM((micro, 2, toks), jnp.int32),
            pltpu.VMEM((micro, toks, width), BF16),
            pltpu.VMEM((micro, toks, width), BF16),
            pltpu.VMEM((width, hidden), BF16),
            pltpu.VMEM((width, hidden), BF16),
            pltpu.VMEM((width, hidden), BF16),
            pltpu.VMEM((n_peer // 2, 16, 1024), BF16),
            pltpu.VMEM((n_x, 2, 16, 1024), BF16),
            pltpu.VMEM((n_x, 4, 16, 1024), BF16),
            pltpu.VMEM((4, 128, 1024), BF16),
            pltpu.VMEM((2, 16, 2, 64, 128), BF16),
            pltpu.VMEM((2, 16, 64, 128), BF16),
            pltpu.VMEM((3, 128, hidden), BF16),
            pltpu.VMEM((3, 128, hidden), BF16),
            pltpu.VMEM((n_x, 4, 16, 1024), BF16),
            pltpu.VMEM((n_peer, 16, 1024), BF16),
            pltpu.VMEM((512, 128), BF16),
            pltpu.VMEM((16, 192, hidden), BF16),
            pltpu.VMEM((4, n_y - 1, 96, hidden), BF16),
            pltpu.VMEM((2, 96, hidden), BF16),
            dma((7,)),
            dma((n_x,)),
            dma((n_x,)),
            dma((n_x,)),
            dma((n_x,)),
            dma((n_x // 2, 2)),
            dma((n_x, 4)),
            dma((n_x, 4)),
            dma((n_peer,)),
            dma((2,)),
            dma((2,)),
            dma((4, n_y - 1)),
            dma((4, n_y - 1)),
            dma((2,)),
            dma((2,)),
        ],
        compiler_params=pltpu.CompilerParams(
            collective_id=0, has_side_effects=True, vmem_limit_bytes=56 * 1024 * 1024
        ),
        name="moe_layer",
    )(
        routes.transpose(0, 2, 1),
        gate_codes.transpose(0, 2, 1),
        tokens,
        cotangent,
        gate_weight,
        up_weight,
        down_weight,
    )
    return pl.pallas_call(
        functools.partial(write_kernel, len(shapes)),
        out_shape=shapes,
        in_specs=[anyspace] * len(shapes),
        out_specs=(hbm,) * len(shapes),
        scratch_shapes=[pltpu.VMEM(one.shape, one.dtype) for one in shapes]
        + [dma((len(shapes),)), dma((len(shapes),))],
        name="write_out",
    )(*results)


def solution(mesh):
    tok_spec = P(None, ("dp", "expert"), None)
    w_spec = P("expert", None, None)
    g_spec = P("expert", "dp", None)
    return jax.shard_map(
        shards,
        mesh=mesh,
        in_specs=(tok_spec,) * 4 + (w_spec,) * 3,
        out_specs=(tok_spec,) * 2 + (g_spec,) * 3,
        check_vma=False,
    )
```

time: 108 us -> 92.1 us (0.85)
  the two profiles are of different devices: /device:TPU:8 before, /device:TPU:20 now
where the time goes in v2:
time: 92.1 us; the launch traced here: 91.9 us
  Pallas kernels  91.3 us (99%)
    pallas_call x1, Pallas kernels, shards(): pl.pallas_call(functools.partial(kernel, scale_factor, n_dp, n_peer), out...  89.5 us

profile of v2, /device:TPU:20, one launch (start us, length us, event | category | flops | bytes accessed | tf_op | source)
XLA Modules:
  0.0 91.9 jit_solution(7278760701012290152)
XLA Ops:
  0.6 89.5 %moe_layer.1 = (bf16[2,8,2048]{2,1,0:T(8,128)(2,1)}, bf16[2,8,2048]{2,1,0:T(8,128)(2,1)}, f32[1,64,384]{2,1,0:T(8,128)}, f32[1,64,384]{2,1,0:T(8,128)}, f32[1,64,384]{2,1,0:T(8,128)}) custom-call(s32[2,2,8]{2,1,0:T(2,128)} %bitcast.2, s32[2,2,8]{2,1,0:T(2,128)} %bitcast.3, bf16[2,8,2048]{2,1,0:T(8,128)(2,1)} %tok_hbm.1, bf16[2,8,2048]{2,1,0:T(8,128)(2,1)} %cot_hbm.1, ...), custom_call_target="tpu_custom_call" | custom-call | tf_op jit(solution)/shard_map/moe_layer/pallas_call | solution.py:530
  90.1 1.8 %write_out.1 = (bf16[2,8,2048]{2,1,0:T(8,128)(2,1)}, bf16[2,8,2048]{2,1,0:T(8,128)(2,1)}, f32[1,64,384]{2,1,0:T(8,128)}, f32[1,64,384]{2,1,0:T(8,128)}, f32[1,64,384]{2,1,0:T(8,128)}) custom-call(bf16[2,8,2048]{2,1,0:T(8,128)(2,1)} %get-tuple-element.10.refs_0_, bf16[2,8,2048]{2,1,0:T(8,128)(2,1)} %get-tuple-element.11.refs_1_, ...), custom_call_target="tpu_custom_call" | custom-call | tf_op jit(solution)/shard_map/write_out/pallas_call | solution.py:586

commit v3 on v2

--- a/solution.py
+++ b/solution.py
@@ -116,10 +116,15 @@
     gs,
     gs_pair,
     retbox,
+    mate_near,
+    mate_far,
+    crossbox,
+    colbox,
     retin,
     comb,
     parts,
     ring,
+    zout,
     zbox,
     w_sem,
     xs_sem,
@@ -128,8 +133,12 @@
     os_sem,
     hs_sem,
     pr_sem,
-    rs_sem,
-    rr_sem,
+    ms_sem,
+    mr_sem,
+    qs_sem,
+    qr_sem,
+    bs_sem,
+    br_sem,
     cs_sem,
     cr_sem,
     ys_sem,
@@ -164,13 +173,14 @@
 
     barrier = pltpu.get_barrier_semaphore()
 
-    def greet(j, carry):
+    for n in range(1, n_x):
         pl.semaphore_signal(
-            barrier, inc=1, device_id={"expert": (k + j) % n_peer}, device_id_type=MESH
-        )
-        return carry
-
-    lax.fori_loop(1, n_peer, greet, 0)
+            barrier, inc=1, device_id={"expert": (x + n) % n_x * 4 + z}, device_id_type=MESH
+        )
+    for n in range(1, 4):
+        pl.semaphore_signal(
+            barrier, inc=1, device_id={"expert": x * 4 + (z + n) % 4}, device_id_type=MESH
+        )
     for other in (pair, zpart, up, down):
         pl.semaphore_signal(barrier, inc=1, device_id={"dp": other}, device_id_type=MESH)
 
@@ -200,7 +210,7 @@
     )
     outbox[...] = (slot_scale * dot(pick, stack)).astype(BF16).reshape(16, 16, 1024)
 
-    pl.semaphore_wait(barrier, n_peer - 1 + 4)
+    pl.semaphore_wait(barrier, n_x - 1 + 3 + 4)
 
     def over_x(at):
         return pltpu.make_async_remote_copy(
@@ -262,7 +272,7 @@
     weight = jnp.where(((lane >> 4) & 1) == 0, all_share, 1.0)
     high = weight.astype(BF16).astype(F32)
     weight = jnp.where(lane < 64, high, weight - high)
-    mask0, mask1 = slot_masks(512, 5, cols, all_lanes)
+    mask0, mask1 = slot_masks(256, 4, cols, all_lanes)
     comb[...] = (
         jnp.where(mask0, weight[0:1, :], 0.0) + jnp.where(mask1, weight[1:2, :], 0.0)
     ).astype(BF16)
@@ -310,6 +320,19 @@
     relay_turn(3)
     sort_rows(2)
     sort_rows(3)
+
+    for q in range(4):
+        turned = jnp.transpose(xs[q])
+        xt[q % 2, (q // 2) * 8 : (q // 2 + 1) * 8] = turned.reshape(8, 2, 64, 128)
+    xt_copy = pltpu.make_async_remote_copy(
+        src_ref=xt.at[:, :, 1 - core],
+        dst_ref=xt_pair,
+        send_sem=cs_sem.at[0],
+        recv_sem=cr_sem.at[0],
+        device_id={"dp": pair},
+        device_id_type=MESH,
+    )
+    xt_copy.start()
 
     for copy in w_copies:
         copy.wait()
@@ -335,126 +358,203 @@
     )
     gs_copy.start()
 
-    for q in range(4):
-        turned = jnp.transpose(xs[q])
-        xt[q % 2, (q // 2) * 8 : (q // 2 + 1) * 8] = turned.reshape(8, 2, 64, 128)
-    xt_copy = pltpu.make_async_remote_copy(
-        src_ref=xt.at[:, :, 1 - core],
-        dst_ref=xt_pair,
-        send_sem=cs_sem.at[0],
-        recv_sem=cr_sem.at[0],
-        device_id={"dp": pair},
-        device_id_type=MESH,
-    )
-    xt_copy.start()
-
-    xt_copy.wait_recv()
-    gs_copy.wait_recv()
-    for n in range(3):
-        a = 0 if n < 2 else 1
-        left = jnp.concatenate(
-            [xt[a, :, core].reshape(1024, 128), xt_pair[a].reshape(1024, 128)], axis=1
-        )
-        right = jnp.concatenate([gs[n], gs_pair[n]], axis=0)
-        part = (dot(left, right) * scale_factor).astype(BF16)
-        parts[:, n * 64 : (n + 1) * 64] = part.reshape(16, 64, 384)
-
-    streams = [(part_at, d) for part_at in range(2) for d in range(2)]
-
-    def own_piece(part_at, d, step):
-        side = 1 - zh if part_at == 0 else zh
-        at = (y + 2 * n_y - 1 - step) % n_y if d == 0 else (y + 1 + step) % n_y
-        return parts.at[at * 2 + side, pl.ds(d * 96, 96)]
-
-    def ring_copy(n, source, step):
-        return pltpu.make_async_remote_copy(
-            src_ref=source,
-            dst_ref=ring.at[n, step],
-            send_sem=ys_sem.at[n, step],
-            recv_sem=yr_sem.at[n, step],
-            device_id={"dp": up if streams[n][1] == 0 else down},
-            device_id_type=MESH,
-        )
-
-    for n, (part_at, d) in enumerate(streams):
-        ring_copy(n, own_piece(part_at, d, 0), 0).start()
-
-    for d in range(2):
+    def outputs(d):
         half = slice(d * 1024, (d + 1) * 1024)
         xs[2 * d] = dot_last(hidden, wd[half]).astype(BF16)
         xs[2 * d + 1] = (dot_last(grad_gate, wg[half]) + dot_last(grad_up, wu[half])).astype(BF16)
+
+    outputs(0)
+
+    xt_copy.wait_recv()
+    gs_copy.wait_recv()
+
+    def make_parts(*steps):
+        pairs = [pl.ds((y + step) % n_y * 2, 2) for step in steps]
+        for n in range(3):
+            a = 0 if n < 2 else 1
+            left = [
+                jnp.concatenate(
+                    [xt[a, two, core].reshape(128, 128), xt_pair[a, two].reshape(128, 128)], axis=1
+                )
+                for two in pairs
+            ]
+            right = jnp.concatenate([gs[n], gs_pair[n]], axis=0)
+            part = (dot(jnp.concatenate(left, axis=0), right) * scale_factor).astype(BF16)
+            for m, two in enumerate(pairs):
+                rows = part[m * 128 : (m + 1) * 128].reshape(2, 64, part.shape[1])
+                parts[two, n * 64 : (n + 1) * 64] = rows
+
+    ways = [(half, d) for half in range(2) for d in range(2)]
+
+    def hops(half, d):
+        return n_y // 2 if half == d else (n_y - 1) // 2
+
+    def own_piece(part, half, step):
+        at = (y + step) % n_y * 2 + (1 - zh if part == 0 else zh)
+        return parts.at[at, pl.ds(half * 96, 96)]
+
+    def ring_copy(part, half, d, step, source=None):
+        slot = ring.at[part, half, d, step]
+        return pltpu.make_async_remote_copy(
+            src_ref=slot if source is None else source,
+            dst_ref=slot,
+            send_sem=ys_sem.at[part, half, d, step],
+            recv_sem=yr_sem.at[part, half, d, step],
+            device_id={"dp": up if d == 0 else down},
+            device_id_type=MESH,
+        )
+
+    def ring_send(part, step):
+        for half, d in ways:
+            left = hops(half, d) - step
+            if left > 0:
+                source = own_piece(part, half, left if d == 0 else n_y - left)
+                if step:
+                    ring_copy(part, half, d, step - 1).wait_recv()
+                    total = ring[part, half, d, step - 1].astype(F32) + source[...].astype(F32)
+                    ring[part, half, d, step - 1] = total.astype(BF16)
+                    source = ring.at[part, half, d, step - 1]
+                ring_copy(part, half, d, step, source).start()
+
+    def ring_total(part, half):
+        total = own_piece(part, half, 0)[...].astype(F32)
+        for d in range(2):
+            ring_copy(part, half, d, hops(half, d) - 1).wait_recv()
+            total = total + ring[part, half, d, hops(half, d) - 1].astype(F32)
+        return total
+
+    make_parts(4, 3, n_y - 3)
+    ring_send(0, 0)
+
+    make_parts(2, n_y - 2)
+    outputs(1)
     back_order = jnp.where(((lane >> 2) & 7) * 16 + (lane >> 5) * 4 + (lane & 3) == row, 1.0, 0.0)
     back_order = back_order.astype(BF16)
     for g in range(n_peer // 8):
         block = jnp.concatenate([xs[q, g * 32 : (g + 1) * 32] for q in range(4)], axis=0)
         retbox[2 * g : 2 * g + 2] = dot(back_order, block).astype(BF16).reshape(2, 4, 16, 1024)
 
-    def ret_copy(at, source):
-        return pltpu.make_async_remote_copy(
-            src_ref=retbox.at[at, source],
-            dst_ref=retin.at[k],
-            send_sem=rs_sem.at[at, source],
-            recv_sem=rr_sem.at[k],
-            device_id={"expert": (x + n_x - ORDER[at]) % n_x * 4 + source},
-            device_id_type=MESH,
-        )
-
-    def ret_recv(source):
-        return pltpu.make_async_remote_copy(
-            src_ref=retin.at[source],
-            dst_ref=retin.at[source],
-            send_sem=rs_sem.at[0, 0],
-            recv_sem=rr_sem.at[source],
-            device_id={"expert": source},
-            device_id_type=MESH,
-        )
-
-    def ret_sends():
-        return [(0, (z + n) % 4) for n in range(1, 4)] + [
-            (at, (z + n) % 4) for at in range(1, n_x) for n in range(4)
-        ]
-
-    for at, source in ret_sends():
-        ret_copy(at, source).start()
-    retin[k] = retbox[0, z]
-
-    def ring_add(n, step):
-        part_at, d = streams[n]
-        ring_copy(n, ring.at[n, step], step).wait_recv()
-        ring[n, step] = (
-            ring[n, step].astype(F32) + own_piece(part_at, d, step + 1)[...].astype(F32)
+    side, odd = z // 2, z % 2
+    far = (1 - side) * 2
+    mate = {"expert": x * 4 + z + 1 - odd * 2}
+
+    def mate_own(turn):
+        return pltpu.make_async_remote_copy(
+            src_ref=retbox.at[pl.ds(2 * turn, 2), z + 1 - odd * 2],
+            dst_ref=mate_near.at[turn],
+            send_sem=ms_sem.at[turn, 0],
+            recv_sem=mr_sem.at[turn, 0],
+            device_id=mate,
+            device_id_type=MESH,
+        )
+
+    def mate_other(turn):
+        return pltpu.make_async_remote_copy(
+            src_ref=retbox.at[2 * turn + 1 - odd, pl.ds(far, 2)],
+            dst_ref=mate_far.at[turn],
+            send_sem=ms_sem.at[turn, 1],
+            recv_sem=mr_sem.at[turn, 1],
+            device_id=mate,
+            device_id_type=MESH,
+        )
+
+    def cross(turn, b):
+        return pltpu.make_async_remote_copy(
+            src_ref=crossbox.at[turn, b],
+            dst_ref=colbox.at[2 * turn + odd, side],
+            send_sem=qs_sem.at[turn, b],
+            recv_sem=qr_sem.at[2 * turn + odd],
+            device_id={"expert": x * 4 + far + b},
+            device_id_type=MESH,
+        )
+
+    def cross_arrival(at):
+        return pltpu.make_async_remote_copy(
+            src_ref=colbox.at[at, 1 - side],
+            dst_ref=colbox.at[at, 1 - side],
+            send_sem=qs_sem.at[0, 0],
+            recv_sem=qr_sem.at[at],
+            device_id=mate,
+            device_id_type=MESH,
+        )
+
+    def home(at):
+        return pltpu.make_async_remote_copy(
+            src_ref=colbox.at[at],
+            dst_ref=retin.at[pl.ds(x * 2, 2)],
+            send_sem=bs_sem.at[at],
+            recv_sem=br_sem.at[at],
+            device_id={"expert": (x + n_x - ORDER[at]) % n_x * 4 + z},
+            device_id_type=MESH,
+        )
+
+    def home_arrival(at):
+        return pltpu.make_async_remote_copy(
+            src_ref=colbox.at[at],
+            dst_ref=retin.at[pl.ds((x + ORDER[at]) % n_x * 2, 2)],
+            send_sem=bs_sem.at[at],
+            recv_sem=br_sem.at[at],
+            device_id=mate,
+            device_id_type=MESH,
+        )
+
+    def sum_turn(turn):
+        mate_own(turn).wait_recv()
+        mate_other(turn).wait_recv()
+        two = pl.ds(2 * turn, 2)
+        colbox[two, side] = (retbox[two, z].astype(F32) + mate_near[turn].astype(F32)).astype(BF16)
+        crossbox[turn] = (
+            retbox[2 * turn + odd, pl.ds(far, 2)].astype(F32) + mate_far[turn].astype(F32)
         ).astype(BF16)
-
-    def ring_step(step, carry):
-        for n in range(4):
-            ring_add(n, step)
-            ring_copy(n, ring.at[n, step], step + 1).start()
-        return carry
-
-    last = n_y - 2
-    lax.fori_loop(0, last, ring_step, 0)
+        for b in range(2):
+            cross(turn, b).start()
+
+    def home_turn(turn):
+        for at in (2 * turn + 1, 2 * turn):
+            cross_arrival(at).wait_recv()
+            if at:
+                home(at).start()
+            else:
+                retin[pl.ds(x * 2, 2)] = colbox[0]
+
+    for turn in (3, 2, 1, 0):
+        mate_other(turn).start()
+        mate_own(turn).start()
 
     z_copies = [
         pltpu.make_async_remote_copy(
-            src_ref=ring.at[d, last],
-            dst_ref=zbox.at[d],
-            send_sem=zs_sem.at[d],
-            recv_sem=zr_sem.at[d],
+            src_ref=zout.at[half],
+            dst_ref=zbox.at[half],
+            send_sem=zs_sem.at[half],
+            recv_sem=zr_sem.at[half],
             device_id={"dp": zpart},
             device_id_type=MESH,
         )
-        for d in range(2)
+        for half in range(2)
     ]
-    for d in range(2):
-        ring_add(d, last)
-        z_copies[d].start()
-
-    def ret_wait(j, carry):
-        ret_recv((k + n_peer - j) % n_peer).wait_recv()
-        return carry
-
-    lax.fori_loop(1, n_peer, ret_wait, 0)
-    both = dot_first(comb[...], retin[...].reshape(512, 1024))
+    ring_send(0, 1)
+    ring_send(1, 0)
+    make_parts(1, n_y - 1, 0)
+    sum_turn(3)
+    ring_send(0, 2)
+    ring_send(1, 1)
+    sum_turn(2)
+    home_turn(3)
+    sum_turn(1)
+    home_turn(2)
+    ring_send(0, 3)
+    ring_send(1, 2)
+    sum_turn(0)
+    home_turn(1)
+    for half in range(2):
+        zout[half] = ring_total(0, half).astype(BF16)
+        z_copies[half].start()
+    ring_send(1, 3)
+
+    home_turn(0)
+    for at in range(n_x - 1, 0, -1):
+        home_arrival(at).wait_recv()
+    both = dot_first(comb[...], retin[...].reshape(256, 1024))
     total = (both[0:64] + both[64:128]).astype(BF16)
     for m in range(2):
         for d in range(2):
@@ -464,12 +564,10 @@
             back_ref[m, :, half] = total[at + 16 : at + 24]
 
     sums = []
-    for d in range(2):
-        n = 2 + d
-        ring_copy(n, ring.at[n, last], last).wait_recv()
-        own = ring[n, last].astype(F32) + own_piece(1, d, last + 1)[...].astype(F32)
-        z_copies[d].wait_recv()
-        sums.append(own + zbox[d].astype(F32))
+    for half in range(2):
+        total = ring_total(1, half)
+        z_copies[half].wait_recv()
+        sums.append(total + zbox[half].astype(F32))
     gg_ref[0] = sums[0][0:64]
     gu_ref[0, 0:32] = sums[0][64:96]
     gu_ref[0, 32:64] = sums[1][0:32]
@@ -483,17 +581,20 @@
     for turn in range(n_x // 2):
         for b in range(2):
             hand_on(turn, b).wait_send()
-    for at, source in ret_sends():
-        ret_copy(at, source).wait_send()
+    for turn in range(n_x // 2):
+        mate_own(turn).wait_send()
+        mate_other(turn).wait_send()
+        for b in range(2):
+            cross(turn, b).wait_send()
+    for at in range(1, n_x):
+        home(at).wait_send()
     xt_copy.wait_send()
     gs_copy.wait_send()
 
-    def ring_wait(step, carry):
-        for n in range(4):
-            ring_copy(n, ring.at[n, step], step).wait_send()
-        return carry
-
-    lax.fori_loop(0, last + 1, ring_wait, 0)
+    for part in range(2):
+        for half, d in ways:
+            for step in range(hops(half, d)):
+                ring_copy(part, half, d, step).wait_send()
     for copy in z_copies:
         copy.wait_send()
 
@@ -549,10 +650,15 @@
             pltpu.VMEM((3, 128, hidden), BF16),
             pltpu.VMEM((3, 128, hidden), BF16),
             pltpu.VMEM((n_x, 4, 16, 1024), BF16),
-            pltpu.VMEM((n_peer, 16, 1024), BF16),
-            pltpu.VMEM((512, 128), BF16),
+            pltpu.VMEM((n_x // 2, 2, 16, 1024), BF16),
+            pltpu.VMEM((n_x // 2, 2, 16, 1024), BF16),
+            pltpu.VMEM((n_x // 2, 2, 16, 1024), BF16),
+            pltpu.VMEM((n_x, 2, 16, 1024), BF16),
+            pltpu.VMEM((n_peer // 2, 16, 1024), BF16),
+            pltpu.VMEM((256, 128), BF16),
             pltpu.VMEM((16, 192, hidden), BF16),
-            pltpu.VMEM((4, n_y - 1, 96, hidden), BF16),
+            pltpu.VMEM((2, 2, 2, n_y // 2, 96, hidden), BF16),
+            pltpu.VMEM((2, 96, hidden), BF16),
             pltpu.VMEM((2, 96, hidden), BF16),
             dma((7,)),
             dma((n_x,)),
@@ -561,12 +667,16 @@
             dma((n_x,)),
             dma((n_x // 2, 2)),
             dma((n_x, 4)),
-            dma((n_x, 4)),
-            dma((n_peer,)),
+            dma((n_x // 2, 2)),
+            dma((n_x // 2, 2)),
+            dma((n_x // 2, 2)),
+            dma((n_x,)),
+            dma((n_x,)),
+            dma((n_x,)),
             dma((2,)),
             dma((2,)),
-            dma((4, n_y - 1)),
-            dma((4, n_y - 1)),
+            dma((2, 2, 2, n_y // 2)),
+            dma((2, 2, 2, n_y // 2)),
             dma((2,)),
             dma((2,)),
         ],

time: 92.1 us -> 85.3 us (0.926)
  the two profiles are of different devices: /device:TPU:20 before, /device:TPU:16 now
where the time goes in v3:
time: 85.3 us; the launch traced here: 85.1 us
  Pallas kernels  84.5 us (99%)
    pallas_call x1, Pallas kernels, shards(): pl.pallas_call(functools.partial(kernel, scale_factor, n_dp, n_peer), out...  82.7 us
    pallas_call x1, Pallas kernels, shards(): pl.pallas_call(functools.partial(write_kernel, len(shapes)), out_shape=sh...  1.79 us

profile of v3, /device:TPU:16, one launch (start us, length us, event | category | flops | bytes accessed | tf_op | source)
XLA Modules:
  0.0 85.1 jit_solution(17251722069673968383)
XLA Ops:
  0.6 82.7 %moe_layer.1 = (bf16[2,8,2048]{2,1,0:T(8,128)(2,1)}, bf16[2,8,2048]{2,1,0:T(8,128)(2,1)}, f32[1,64,384]{2,1,0:T(8,128)}, f32[1,64,384]{2,1,0:T(8,128)}, f32[1,64,384]{2,1,0:T(8,128)}) custom-call(s32[2,2,8]{2,1,0:T(2,128)} %bitcast.2, s32[2,2,8]{2,1,0:T(2,128)} %bitcast.3, bf16[2,8,2048]{2,1,0:T(8,128)(2,1)} %tok_hbm.1, bf16[2,8,2048]{2,1,0:T(8,128)(2,1)} %cot_hbm.1, ...), custom_call_target="tpu_custom_call" | custom-call | tf_op jit(solution)/shard_map/moe_layer/pallas_call | solution.py:631
  83.3 1.8 %write_out.1 = (bf16[2,8,2048]{2,1,0:T(8,128)(2,1)}, bf16[2,8,2048]{2,1,0:T(8,128)(2,1)}, f32[1,64,384]{2,1,0:T(8,128)}, f32[1,64,384]{2,1,0:T(8,128)}, f32[1,64,384]{2,1,0:T(8,128)}) custom-call(bf16[2,8,2048]{2,1,0:T(8,128)(2,1)} %get-tuple-element.10.refs_0_, bf16[2,8,2048]{2,1,0:T(8,128)(2,1)} %get-tuple-element.11.refs_1_, ...), custom_call_target="tpu_custom_call" | custom-call | tf_op jit(solution)/shard_map/write_out/pallas_call | solution.py:696

commit v4 on v3

--- a/solution.py
+++ b/solution.py
@@ -285,8 +285,8 @@
     def forward(at):
         if at:
             over_x(at).wait_recv()
+        to_other(at).start()
         to_pair(at).start()
-        to_other(at).start()
         inbox[at, z] = relay[at, z // 2]
 
     def relay_turn(turn):
@@ -313,9 +313,9 @@
     relay_turn(1)
     forward(5)
     forward(6)
-    relay_turn(2)
     sort_rows(0)
     forward(7)
+    relay_turn(2)
     sort_rows(1)
     relay_turn(3)
     sort_rows(2)
@@ -363,7 +363,6 @@
         xs[2 * d] = dot_last(hidden, wd[half]).astype(BF16)
         xs[2 * d + 1] = (dot_last(grad_gate, wg[half]) + dot_last(grad_up, wu[half])).astype(BF16)
 
-    outputs(0)
 
     xt_copy.wait_recv()
     gs_copy.wait_recv()
@@ -426,6 +425,7 @@
     make_parts(4, 3, n_y - 3)
     ring_send(0, 0)
 
+    outputs(0)
     make_parts(2, n_y - 2)
     outputs(1)
     back_order = jnp.where(((lane >> 2) & 7) * 16 + (lane >> 5) * 4 + (lane & 3) == row, 1.0, 0.0)

time: 85.3 us -> 80.1 us (0.939)
  the two profiles are of different devices: /device:TPU:16 before, /device:TPU:257 now
where the time goes in v4:
time: 80.1 us; the launch traced here: 80 us
  Pallas kernels  79.3 us (99%)
    pallas_call x1, Pallas kernels, shards(): pl.pallas_call(functools.partial(kernel, scale_factor, n_dp, n_peer), out...  77.5 us
    pallas_call x1, Pallas kernels, shards(): pl.pallas_call(functools.partial(write_kernel, len(shapes)), out_shape=sh...  1.79 us

profile of v4, /device:TPU:257, one launch (start us, length us, event | category | flops | bytes accessed | tf_op | source)
XLA Modules:
  0.0 80.0 jit_solution(12009058379292541386)
XLA Ops:
  0.6 77.5 %moe_layer.1 = (bf16[2,8,2048]{2,1,0:T(8,128)(2,1)}, bf16[2,8,2048]{2,1,0:T(8,128)(2,1)}, f32[1,64,384]{2,1,0:T(8,128)}, f32[1,64,384]{2,1,0:T(8,128)}, f32[1,64,384]{2,1,0:T(8,128)}) custom-call(s32[2,2,8]{2,1,0:T(2,128)} %bitcast.2, s32[2,2,8]{2,1,0:T(2,128)} %bitcast.3, bf16[2,8,2048]{2,1,0:T(8,128)(2,1)} %tok_hbm.1, bf16[2,8,2048]{2,1,0:T(8,128)(2,1)} %cot_hbm.1, ...), custom_call_target="tpu_custom_call" | custom-call | tf_op jit(solution)/shard_map/moe_layer/pallas_call | solution.py:631
  78.2 1.8 %write_out.1 = (bf16[2,8,2048]{2,1,0:T(8,128)(2,1)}, bf16[2,8,2048]{2,1,0:T(8,128)(2,1)}, f32[1,64,384]{2,1,0:T(8,128)}, f32[1,64,384]{2,1,0:T(8,128)}, f32[1,64,384]{2,1,0:T(8,128)}) custom-call(bf16[2,8,2048]{2,1,0:T(8,128)(2,1)} %get-tuple-element.10.refs_0_, bf16[2,8,2048]{2,1,0:T(8,128)(2,1)} %get-tuple-element.11.refs_1_, ...), custom_call_target="tpu_custom_call" | custom-call | tf_op jit(solution)/shard_map/write_out/pallas_call | solution.py:696

commit v5 on v4

--- a/solution.py
+++ b/solution.py
@@ -111,6 +111,7 @@
     relay,
     inbox,
     xs,
+    yt,
     xt,
     xt_pair,
     gs,
@@ -264,19 +265,6 @@
             device_id_type=MESH,
         )
 
-    for at in range(1, n_x):
-        over_x(at).start()
-    relay[0] = outbox[pl.ds(x * 2, 2)]
-
-    lane = iota((2, 128), 1)
-    weight = jnp.where(((lane >> 4) & 1) == 0, all_share, 1.0)
-    high = weight.astype(BF16).astype(F32)
-    weight = jnp.where(lane < 64, high, weight - high)
-    mask0, mask1 = slot_masks(256, 4, cols, all_lanes)
-    comb[...] = (
-        jnp.where(mask0, weight[0:1, :], 0.0) + jnp.where(mask1, weight[1:2, :], 0.0)
-    ).astype(BF16)
-
     row = iota((128, 128), 0)
     lane = iota((128, 128), 1)
     order = jnp.where(((row >> 2) & 7) * 16 + (row >> 5) * 4 + (row & 3) == lane, 1.0, 0.0)
@@ -304,9 +292,24 @@
         for q in range(4):
             xs[q, g * 32 : (g + 1) * 32] = sorted_rows[q * 32 : (q + 1) * 32]
 
+    relay[0] = outbox[pl.ds(x * 2, 2)]
+    over_x(1).start()
+    over_x(2).start()
     forward(0)
+    for at in range(3, n_x):
+        over_x(at).start()
     forward(1)
     forward(2)
+
+    along = iota((2, 128), 1)
+    weight = jnp.where(((along >> 4) & 1) == 0, all_share, 1.0)
+    high = weight.astype(BF16).astype(F32)
+    weight = jnp.where(along < 64, high, weight - high)
+    mask0, mask1 = slot_masks(256, 4, cols, all_lanes)
+    comb[...] = (
+        jnp.where(mask0, weight[0:1, :], 0.0) + jnp.where(mask1, weight[1:2, :], 0.0)
+    ).astype(BF16)
+
     relay_turn(0)
     forward(3)
     forward(4)
@@ -360,9 +363,10 @@
 
     def outputs(d):
         half = slice(d * 1024, (d + 1) * 1024)
-        xs[2 * d] = dot_last(hidden, wd[half]).astype(BF16)
-        xs[2 * d + 1] = (dot_last(grad_gate, wg[half]) + dot_last(grad_up, wu[half])).astype(BF16)
-
+        yt[:, d * 256 : d * 256 + 128] = dot(wd[half], turned_hidden).astype(BF16)
+        yt[:, d * 256 + 128 : d * 256 + 256] = (
+            dot(wg[half], turned_gate) + dot(wu[half], turned_up)
+        ).astype(BF16)
 
     xt_copy.wait_recv()
     gs_copy.wait_recv()
@@ -425,14 +429,19 @@
     make_parts(4, 3, n_y - 3)
     ring_send(0, 0)
 
+    turned_hidden = jnp.transpose(hidden)
+    turned_gate = jnp.transpose(grad_gate)
+    turned_up = jnp.transpose(grad_up)
     outputs(0)
-    make_parts(2, n_y - 2)
     outputs(1)
-    back_order = jnp.where(((lane >> 2) & 7) * 16 + (lane >> 5) * 4 + (lane & 3) == row, 1.0, 0.0)
+    row = iota((512, 512), 0)
+    lane = iota((512, 512), 1)
+    back_order = jnp.where(((row >> 2) & 3) * 128 + (row >> 4) * 4 + (row & 3) == lane, 1.0, 0.0)
     back_order = back_order.astype(BF16)
-    for g in range(n_peer // 8):
-        block = jnp.concatenate([xs[q, g * 32 : (g + 1) * 32] for q in range(4)], axis=0)
-        retbox[2 * g : 2 * g + 2] = dot(back_order, block).astype(BF16).reshape(2, 4, 16, 1024)
+    for h in range(2):
+        half = slice(h * 512, (h + 1) * 512)
+        block = dot_last(back_order, yt[half]).astype(BF16)
+        retbox[:, :, :, half] = block.reshape(n_x, 4, 16, 512)
 
     side, odd = z // 2, z % 2
     far = (1 - side) * 2
@@ -520,6 +529,7 @@
     for turn in (3, 2, 1, 0):
         mate_other(turn).start()
         mate_own(turn).start()
+    make_parts(2, n_y - 2)
 
     z_copies = [
         pltpu.make_async_remote_copy(
@@ -645,6 +655,7 @@
             pltpu.VMEM((n_x, 2, 16, 1024), BF16),
             pltpu.VMEM((n_x, 4, 16, 1024), BF16),
             pltpu.VMEM((4, 128, 1024), BF16),
+            pltpu.VMEM((1024, 512), BF16),
             pltpu.VMEM((2, 16, 2, 64, 128), BF16),
             pltpu.VMEM((2, 16, 64, 128), BF16),
             pltpu.VMEM((3, 128, hidden), BF16),

time: 80.1 us -> 80 us (level)
  no operation moved by 1% of the time
where the time goes in v5:
time: 80 us; the launch traced here: 79.8 us
  Pallas kernels  79.2 us (99%)
    pallas_call x1, Pallas kernels, shards(): pl.pallas_call(functools.partial(kernel, scale_factor, n_dp, n_peer), out...  77.4 us
    pallas_call x1, Pallas kernels, shards(): pl.pallas_call(functools.partial(write_kernel, len(shapes)), out_shape=sh...  1.79 us

profile of v5, /device:TPU:257, one launch (start us, length us, event | category | flops | bytes accessed | tf_op | source)
XLA Modules:
  0.0 79.8 jit_solution(8139888186706894240)
XLA Ops:
  0.6 77.4 %moe_layer.1 = (bf16[2,8,2048]{2,1,0:T(8,128)(2,1)}, bf16[2,8,2048]{2,1,0:T(8,128)(2,1)}, f32[1,64,384]{2,1,0:T(8,128)}, f32[1,64,384]{2,1,0:T(8,128)}, f32[1,64,384]{2,1,0:T(8,128)}) custom-call(s32[2,2,8]{2,1,0:T(2,128)} %bitcast.2, s32[2,2,8]{2,1,0:T(2,128)} %bitcast.3, bf16[2,8,2048]{2,1,0:T(8,128)(2,1)} %tok_hbm.1, bf16[2,8,2048]{2,1,0:T(8,128)(2,1)} %cot_hbm.1, ...), custom_call_target="tpu_custom_call" | custom-call | tf_op jit(solution)/shard_map/moe_layer/pallas_call | solution.py:641
  78.0 1.8 %write_out.1 = (bf16[2,8,2048]{2,1,0:T(8,128)(2,1)}, bf16[2,8,2048]{2,1,0:T(8,128)(2,1)}, f32[1,64,384]{2,1,0:T(8,128)}, f32[1,64,384]{2,1,0:T(8,128)}, f32[1,64,384]{2,1,0:T(8,128)}) custom-call(bf16[2,8,2048]{2,1,0:T(8,128)(2,1)} %get-tuple-element.10.refs_0_, bf16[2,8,2048]{2,1,0:T(8,128)(2,1)} %get-tuple-element.11.refs_1_, ...), custom_call_target="tpu_custom_call" | custom-call | tf_op jit(solution)/shard_map/write_out/pallas_call | solution.py:707
